TPU v7x, 256 devices: a whole 4x4x8 slice. The times are simulated.
256 devices in a mesh: sec: 32 (over z, x_lo, core), tp: 8 (over x_hi, y).
Axes of the slice: x: 4 (x_hi: 2, x_lo: 2; x = x_hi * 2 + x_lo), y: 4, z: 8, core: 2. Of those that a mesh axis runs over, the one named last changes fastest.
Arguments:
- patches: bfloat16 [1024, 5120], P('sec', 'tp'), may hold values from -6 to 6
- merge_gain: float32 [1280], replicated, may hold values from 0.5 to 1.5
- merge_bias: float32 [1280], replicated, may hold values from -2 to 2
- merge_inner: bfloat16 [5120, 3072], P(None, 'tp'), may hold values from -0.078125 to 0.078125
- merge_outer: bfloat16 [3072, 8192], P('tp'), may hold values from -0.109375 to 0.109375
- slot_target: int32 [1024], replicated, may hold values from 0 to 4095, as said below
- text_embed: bfloat16 [2, 2048, 8192], P(None, 'sec', 'tp'), may hold values from -10 to 10
- norm_gain: float32 [8192], replicated, may hold values from 0.5 to 1.5
- query_weight: bfloat16 [8192, 4096], P('sec', 'tp'), may hold values from -0.03691997 to 0.03691997
- key_weight: bfloat16 [8192, 1024], P('sec', 'tp'), may hold values from -0.03691997 to 0.03691997
- value_weight: bfloat16 [8192, 1024], P('sec', 'tp'), may hold values from -0.0625 to 0.0625
- attn_cotangent: bfloat16 [2, 2048, 4096], P(None, 'sec', 'tp'), may hold values from -6 to 6
Outputs:
- attended: bfloat16 [2, 2048, 4096], P(None, 'sec', 'tp')
- grad_text: bfloat16 [2, 2048, 8192], P(None, 'sec', 'tp')
- grad_image: bfloat16 [1024, 8192], P('sec', 'tp')
Inputs may be any that keep to these rules, and one draw needn't show every extreme that they name: `slot_target`: all values differ. Of the 64 positions of each micro-batch on each index of sec, exactly 16 are image places.
All inputs are finite; a program needn't handle non-finite values.
Results may differ from a plain program's by a relative error of at most 0.022.
Values may be sent and summed in bfloat16 or wider, within the bound.
A program may use at most 128 MiB of HBM per device.

v0:
```python
import math

import jax
import jax.numpy as jnp
from jax import lax
from jax.sharding import PartitionSpec as P

HEADS = 32
KV_HEADS = 8
HEAD_DIM = 128


def merge_rows(full_rows, merge_gain, merge_bias, merge_inner, merge_outer):
    row_count = full_rows.shape[0]
    pieces = full_rows.astype(jnp.float32).reshape(row_count, -1, merge_gain.shape[0])
    centre = jnp.mean(pieces, axis=-1, keepdims=True)
    shifted = pieces - centre
    spread = jnp.mean(shifted * shifted, axis=-1, keepdims=True)
    normed = (
        (shifted * lax.rsqrt(spread + 1e-06) * merge_gain + merge_bias)
        .reshape(row_count, -1)
        .astype(jnp.bfloat16)
    )
    hidden = jax.nn.gelu(
        jnp.dot(normed, merge_inner, preferred_element_type=jnp.float32), approximate=False
    ).astype(jnp.bfloat16)
    return jnp.dot(hidden, merge_outer, preferred_element_type=jnp.float32)


def pick_rows(wanted, current, block_rows):
    inside = (wanted >= 0) & (wanted < block_rows.shape[0])
    chosen = jnp.take(block_rows, jnp.clip(wanted, 0, block_rows.shape[0] - 1), axis=0)
    return jnp.where(inside[..., None], chosen, current)


def per_device(
    patches,
    merge_gain,
    merge_bias,
    merge_inner,
    merge_outer,
    slot_target,
    text_embed,
    norm_gain,
    query_weight,
    key_weight,
    value_weight,
    attn_cotangent,
):
    sec_count = lax.axis_size("sec")
    sec_index = lax.axis_index("sec")
    micro_count, tok_local, feat_local = text_embed.shape
    seq_len = tok_local * sec_count
    slot_total = slot_target.shape[0]
    rows_local = slot_total // sec_count
    places = micro_count * seq_len
    source = (
        jnp.full((places,), -1, jnp.int32)
        .at[slot_target]
        .set(jnp.arange(slot_total, dtype=jnp.int32))
    )
    batch_ids = jnp.arange(micro_count, dtype=jnp.int32)
    local_ids = jnp.arange(tok_local, dtype=jnp.int32)
    my_places = batch_ids[:, None] * seq_len + sec_index * tok_local + local_ids[None, :]
    my_source = jnp.take(source, my_places)
    is_image = my_source >= 0
    flat_mask = is_image.reshape(-1).astype(jnp.int32)
    compact_index = jnp.argsort(1 - flat_mask, stable=True)[:rows_local]
    owner_major = (
        (source >= 0)
        .astype(jnp.int32)
        .reshape(micro_count, sec_count, tok_local)
        .transpose(1, 0, 2)
        .reshape(-1)
    )
    rank_order = jnp.cumsum(owner_major) - 1
    rank_grid = rank_order.reshape(sec_count, micro_count, tok_local).transpose(1, 0, 2).reshape(-1)
    my_slots = lax.dynamic_slice_in_dim(slot_target, sec_index * rows_local, rows_local)
    return_index = jnp.take(rank_grid, my_slots)
    full_rows = lax.all_gather(patches, "tp", axis=1, tiled=True)
    partial_value = merge_rows(full_rows, merge_gain, merge_bias, merge_inner, merge_outer)
    image_embed = lax.psum_scatter(partial_value, "tp", scatter_dimension=1, tiled=True).astype(
        jnp.bfloat16
    )
    blank_rows = jnp.zeros((micro_count, tok_local, feat_local), jnp.bfloat16)
    image_in = pick_rows(
        my_source, blank_rows, lax.all_gather(image_embed, "sec", axis=0, tiled=True)
    )
    llm_part = jnp.where(is_image[..., None], image_in, text_embed)
    gathered_input = lax.all_gather(llm_part, "tp", axis=2, tiled=True)
    model_width = gathered_input.shape[2]
    input_wide = gathered_input.astype(jnp.float32)
    inv_rms = lax.rsqrt(jnp.mean(input_wide * input_wide, axis=-1, keepdims=True) + 1e-06)
    normed = (input_wide * inv_rms * norm_gain).astype(jnp.bfloat16).reshape(-1, model_width)
    query_full, key_full, value_full = (
        lax.all_gather(query_weight, "sec", axis=0, tiled=True),
        lax.all_gather(key_weight, "sec", axis=0, tiled=True),
        lax.all_gather(value_weight, "sec", axis=0, tiled=True),
    )
    group_size = HEADS // KV_HEADS
    heads_local = key_full.shape[1] // HEAD_DIM
    queries = jnp.dot(normed, query_full, preferred_element_type=jnp.float32).astype(jnp.bfloat16)
    queries = queries.reshape(micro_count, tok_local, heads_local, group_size, HEAD_DIM)
    keys_mine = jnp.dot(normed, key_full, preferred_element_type=jnp.float32).astype(jnp.bfloat16)
    keys_mine = keys_mine.reshape(micro_count, tok_local, heads_local, HEAD_DIM)
    values_mine = jnp.dot(normed, value_full, preferred_element_type=jnp.float32).astype(
        jnp.bfloat16
    )
    values_mine = values_mine.reshape(micro_count, tok_local, heads_local, HEAD_DIM)
    keys_all, values_all = (
        lax.all_gather(keys_mine, "sec", axis=1, tiled=True),
        lax.all_gather(values_mine, "sec", axis=1, tiled=True),
    )
    score_scale = 1.0 / math.sqrt(HEAD_DIM)
    scores = (
        jnp.einsum("msegd,mted->megst", queries, keys_all, preferred_element_type=jnp.float32)
        * score_scale
    )
    query_pos = sec_index * tok_local + local_ids
    key_pos = jnp.arange(seq_len, dtype=jnp.int32)
    allowed = key_pos[None, :] <= query_pos[:, None]
    scores = jnp.where(allowed, scores, -1e30)
    row_max = jnp.max(scores, axis=-1, keepdims=True)
    raw_weights = jnp.exp(scores - row_max)
    attention_weights = raw_weights / jnp.sum(raw_weights, axis=-1, keepdims=True)
    weights_half = attention_weights.astype(jnp.bfloat16)
    attended = jnp.einsum(
        "megst,mted->msegd", weights_half, values_all, preferred_element_type=jnp.float32
    ).astype(jnp.bfloat16)
    attended = attended.reshape(micro_count, tok_local, -1)
    grad_out = attn_cotangent.reshape(micro_count, tok_local, heads_local, group_size, HEAD_DIM)
    grad_weights = jnp.einsum(
        "msegd,mted->megst", grad_out, values_all, preferred_element_type=jnp.float32
    )
    row_delta = jnp.sum(attention_weights * grad_weights, axis=-1, keepdims=True)
    grad_scores = (attention_weights * (grad_weights - row_delta)).astype(jnp.bfloat16)
    grad_q = (
        jnp.einsum("megst,mted->msegd", grad_scores, keys_all, preferred_element_type=jnp.float32)
        * score_scale
    )
    grad_q = grad_q.astype(jnp.bfloat16).reshape(-1, query_full.shape[1])
    key_term = (
        jnp.einsum("megst,msegd->mted", grad_scores, queries, preferred_element_type=jnp.float32)
        * score_scale
    )
    value_term = jnp.einsum(
        "megst,msegd->mted", weights_half, grad_out, preferred_element_type=jnp.float32
    )
    grad_k, grad_v = (
        lax.psum_scatter(
            key_term.astype(jnp.bfloat16), "sec", scatter_dimension=1, tiled=True
        ).astype(jnp.float32),
        lax.psum_scatter(
            value_term.astype(jnp.bfloat16), "sec", scatter_dimension=1, tiled=True
        ).astype(jnp.float32),
    )
    grad_k = grad_k.astype(jnp.bfloat16).reshape(-1, key_full.shape[1])
    grad_v = grad_v.astype(jnp.bfloat16).reshape(-1, value_full.shape[1])
    grad_part = jnp.dot(grad_q, query_full.T, preferred_element_type=jnp.float32)
    grad_part = grad_part + jnp.dot(grad_k, key_full.T, preferred_element_type=jnp.float32)
    grad_part = grad_part + jnp.dot(grad_v, value_full.T, preferred_element_type=jnp.float32)
    grad_part = grad_part.reshape(micro_count, tok_local, model_width)
    tp_start = lax.axis_index("tp") * feat_local
    input_mine = llm_part.astype(jnp.float32)
    grad_full = lax.psum(grad_part.astype(jnp.bfloat16), "tp").astype(jnp.float32)
    scaled_full = grad_full * norm_gain
    inner_sum = jnp.sum(scaled_full * input_wide, axis=-1, keepdims=True)
    scaled = lax.dynamic_slice_in_dim(scaled_full, tp_start, feat_local, 2)
    grad_input = (inv_rms * scaled - input_mine * inv_rms**3 * inner_sum / model_width).astype(
        jnp.bfloat16
    )
    grad_text = jnp.where(is_image[..., None], jnp.zeros_like(grad_input), grad_input)
    compact_grads = jnp.take(grad_input.reshape(-1, feat_local), compact_index, axis=0)
    blank_grads = jnp.zeros((rows_local, feat_local), jnp.bfloat16)
    grad_image = pick_rows(
        return_index, blank_grads, lax.all_gather(compact_grads, "sec", axis=0, tiled=True)
    )
    return (attended, grad_text, grad_image)


def solution(mesh):
    return jax.shard_map(
        per_device,
        mesh=mesh,
        in_specs=(
            P("sec", "tp"),
            P(),
            P(),
            P(None, "tp"),
            P("tp", None),
            P(),
            P(None, "sec", "tp"),
            P(),
            P("sec", "tp"),
            P("sec", "tp"),
            P("sec", "tp"),
            P(None, "sec", "tp"),
        ),
        out_specs=(P(None, "sec", "tp"), P(None, "sec", "tp"), P("sec", "tp")),
        check_vma=False,
    )
```

profile of v0, /device:TPU:1, one launch (start us, length us, event | category | flops | bytes accessed | tf_op | source)
XLA Modules:
  0.0 1130.6 jit_solution(17175009292700798211)
XLA Ops:
  7.2 30.0 %all_gather.27 = bf16[32,5120]{1,0:T(8,128)(2,1)S(1)} all-gather(bf16[32,640]{1,0:T(8,128)(2,1)} %param.12), channel_id=1, replica_groups=mesh['sec'=32,'tp'=8] {'tp'}, dimensions={1}, use_global_device_ids=true | all-gather | bytes 368640 | tf_op jit(solution)/shard_map/all_gather | solution.py:80
  38.8 6.9 fusion.57
  45.8 83.5 %reduce-scatter.3.cloned.1.call-done = f32[32,1024]{1,0:T(8,128)} async-done(((f32[32,8192]{1,0:T(8,128)}), f32[32,1024]{1,0:T(8,128)}) %reduce-scatter.3.cloned.1.call-update) | async-done | bytes 131088 | tf_op jit(solution)/shard_map/reduce_scatter | solution.py:82
  131.0 4.3 scatter_custom_fusion
  137.0 60.9 %all-gather.9.cloned.1.call-done = bf16[1024,1024]{1,0:T(8,128)(2,1)} async-done(((bf16[32,1024]{1,0:T(8,128)(2,1)}), bf16[1024,1024]{1,0:T(8,128)(2,1)}) %all-gather.9.cloned.1.call-update) | async-done | bytes 2097168 | tf_op jit(solution)/shard_map/all_gather | solution.py:87
  197.9 2.9 gather_fusion.1
  203.5 56.3 %all-gather.11.cloned.1.call-done = bf16[2,64,8192]{2,1,0:T(8,128)(2,1)} async-done(((bf16[2,64,1024]{2,1,0:T(8,128)(2,1)}), bf16[2,64,8192]{2,1,0:T(8,128)(2,1)}) %all-gather.11.cloned.1.call-update) | async-done | bytes 2097168 | tf_op jit(solution)/shard_map/all_gather | solution.py:90
  259.8 2.1 fusion.1
  261.9 2.2 fusion.3
  264.1 61.0 %all-gather.17.cloned.1.call-done = bf16[8192,128]{1,0:T(8,128)(2,1)} async-done(((bf16[256,128]{1,0:T(8,128)(2,1)}), bf16[8192,128]{1,0:T(8,128)(2,1)}) %all-gather.17.cloned.1.call-update) | async-done | bytes 2097168 | tf_op jit(solution)/shard_map/all_gather | solution.py:97
  325.1 2.9 convolution_convert_fusion.1
  328.0 63.3 %all-gather.13.cloned.1.call-done = bf16[8192,128]{1,0:T(8,128)(2,1)} async-done(((bf16[256,128]{1,0:T(8,128)(2,1)}), bf16[8192,128]{1,0:T(8,128)(2,1)}) %all-gather.13.cloned.1.call-update) | async-done | bytes 2097168 | tf_op jit(solution)/shard_map/all_gather | solution.py:98
  391.3 2.9 convolution_convert_fusion.2
  394.7 70.6 %all-gather.21.cloned.1.call-done = bf16[8192,512]{1,0:T(8,128)(2,1)} async-done(((bf16[256,512]{1,0:T(8,128)(2,1)}), bf16[8192,512]{1,0:T(8,128)(2,1)}) %all-gather.21.cloned.1.call-update) | async-done | bytes 8388624 | tf_op jit(solution)/shard_map/all_gather | solution.py:96
  465.3 4.6 convolution_convert_fusion
  469.9 61.4 %all-gather.19.cloned.1.call-done = bf16[2,2048,1,128]{3,1,0,2:T(8,128)(2,1)} async-done(((bf16[2,64,1,128]{3,1,0,2:T(8,128)(2,1)}), bf16[2,2048,1,128]{3,1,0,2:T(8,128)(2,1)}) %all-gather.19.cloned.1.call-update) | async-done | bytes 1048592 | tf_op jit(solution)/shard_map/all_gather | solution.py:111
  531.4 2.2 fusion.126
  536.2 61.1 %all-gather.15.cloned.1.call-done = bf16[2,2048,1,128]{3,1,0,2:T(8,128)(2,1)} async-done(((bf16[2,64,1,128]{3,1,0,2:T(8,128)(2,1)}), bf16[2,2048,1,128]{3,1,0,2:T(8,128)(2,1)}) %all-gather.15.cloned.1.call-update) | async-done | bytes 1048592 | tf_op jit(solution)/shard_map/all_gather | solution.py:112
  597.3 3.9 fusion.5
  603.0 2.0 copy.41
  605.1 4.6 fusion.14
  611.8 8.3 fusion.38
  620.1 211.2 %all-reduce.6.cloned.1.call-done = bf16[2,2048,1,128]{3,0,2,1:T(2,128)(2,1)} async-done(((bf16[2,2048,1,128]{3,0,2,1:T(2,128)(2,1)}), bf16[2,2048,1,128]{3,0,2,1:T(2,128)(2,1)}) %all-reduce.6.cloned.1.call-update) | async-done | bytes 1048592
  832.1 4.8 convolution_add_fusion.1
  836.9 110.0 %reduce-scatter.5.cloned.1.call-done = bf16[2,64,1,128]{3,1,0,2:T(8,128)(2,1)} async-done(((bf16[2,2048,1,128]{3,1,0,2:T(8,128)(2,1)}), bf16[2,64,1,128]{3,1,0,2:T(8,128)(2,1)}) %reduce-scatter.5.cloned.1.call-update) | async-done | bytes 32784 | tf_op jit(solution)/shard_map/reduce_scatter | solution.py:153
  947.0 5.0 fusion
  952.6 2.5 sort.17
  955.1 91.9 %all-reduce.4.cloned.1.call-done = bf16[2,64,8192]{2,1,0:T(8,128)(2,1)} async-done(((bf16[2,64,8192]{2,1,0:T(8,128)(2,1)}), bf16[2,64,8192]{2,1,0:T(8,128)(2,1)}) %all-reduce.4.cloned.1.call-update) | async-done | bytes 2097168 | tf_op jit(solution)/shard_map/psum | solution.py:165
  1047.1 2.4 convert_multiply_fusion.3
  1053.7 3.3 fusion.23
  1057.8 62.6 %all-gather.23.cloned.1.call-done = bf16[1024,1024]{1,0:T(8,128)(2,1)} async-done(((bf16[32,1024]{1,0:T(8,128)(2,1)}), bf16[1024,1024]{1,0:T(8,128)(2,1)}) %all-gather.23.cloned.1.call-update) | async-done | bytes 2097168 | tf_op jit(solution)/shard_map/all_gather | solution.py:176
  1120.5 2.5 gather_fusion.4
  (124 shorter events, 20.9 us)
Async XLA Ops:
  7.2 590.2 %copy-start = (bf16[2,64,512]{2,1,0:T(8,128)(2,1)S(1)}, bf16[2,64,512]{2,1,0:T(8,128)(2,1)}, u32[]{:S(2)}) copy-start(bf16[2,64,512]{2,1,0:T(8,128)(2,1)} %param.23) | copy-start | bytes 393220
  7.2 31.5 %copy-start.10 = (f32[1280]{0:T(1024)S(1)}, f32[1280]{0:T(1024)}, u32[]{:S(2)}) copy-start(f32[1280]{0:T(1024)} %param.14) | copy-start | bytes 15364
  7.2 31.5 %copy-start.11 = (f32[1280]{0:T(1024)S(1)}, f32[1280]{0:T(1024)}, u32[]{:S(2)}) copy-start(f32[1280]{0:T(1024)} %param.13) | copy-start | bytes 15364
  7.2 122.0 %reduce-scatter.3.cloned.1.call-start = ((), (), s32[]{:S(2)}) async-start(), calls=%async_computation.2 | async-start | bytes 1179648 | tf_op jit(solution)/shard_map/reduce_scatter | solution.py:82
  38.8 92.3 %copy-start.12 = (s32[1024]{0:T(1024)S(1)}, s32[1024]{0:T(1024)}, u32[]{:S(2)}) copy-start(s32[1024]{0:T(1024)} %param.17) | copy-start | bytes 12292
  45.7 155.1 %copy-start.8 = (bf16[2,64,1024]{2,1,0:T(8,128)(2,1)S(1)}, bf16[2,64,1024]{2,1,0:T(8,128)(2,1)}, u32[]{:S(2)}) copy-start(bf16[2,64,1024]{2,1,0:T(8,128)(2,1)} %param.18) | copy-start | bytes 786436
  45.7 216.2 %copy-start.9 = (f32[8192]{0:T(1024)S(1)}, f32[8192]{0:T(1024)}, u32[]{:S(2)}) copy-start(f32[8192]{0:T(1024)} %param.19) | copy-start | bytes 98308
  45.7 152.2 %all-gather.9.cloned.1.call-start = ((), (), s32[]{:S(2)}) async-start(), calls=%async_computation.3 | async-start | bytes 2162688 | tf_op jit(solution)/shard_map/all_gather | solution.py:87
  130.8 128.9 %all-gather.11.cloned.1.call-start = ((), (), s32[]{:S(2)}) async-start(), calls=%async_computation.4 | async-start | bytes 2359296 | tf_op jit(solution)/shard_map/all_gather | solution.py:90
  201.7 123.4 %all-gather.17.cloned.1.call-start = ((), (), s32[]{:S(2)}) async-start(), calls=%async_computation.7 | async-start | bytes 2162688 | tf_op jit(solution)/shard_map/all_gather | solution.py:97
  202.2 189.1 %all-gather.13.cloned.1.call-start = ((), (), s32[]{:S(2)}) async-start(), calls=%async_computation.5 | async-start | bytes 2162688 | tf_op jit(solution)/shard_map/all_gather | solution.py:98
  202.8 262.4 %all-gather.21.cloned.1.call-start = ((), (), s32[]{:S(2)}) async-start(), calls=%async_computation.9 | async-start | bytes 8650752 | tf_op jit(solution)/shard_map/all_gather | solution.py:96
  203.4 327.9 %all-gather.19.cloned.1.call-start = ((), (), s32[]{:S(2)}) async-start(), calls=%async_computation.8 | async-start | bytes 1081344 | tf_op jit(solution)/shard_map/all_gather | solution.py:111
  328.0 269.3 %all-gather.15.cloned.1.call-start = ((), (), s32[]{:S(2)}) async-start(), calls=%async_computation.6 | async-start | bytes 1081344 | tf_op jit(solution)/shard_map/all_gather | solution.py:112
  394.3 437.0 %all-reduce.6.cloned.1.call-start = ((), (), s32[]{:S(2)}) async-start(), calls=%async_computation.13 | async-start | bytes 2097152
  533.5 2.0 copy-start.2
  597.3 3.9 copy-start.3
  605.0 4.7 copy-start.13
  605.0 6.0 copy-start.6
  605.0 342.0 %reduce-scatter.5.cloned.1.call-start = ((), (), s32[]{:S(2)}) async-start(), calls=%async_computation.10 | async-start | bytes 1081344 | tf_op jit(solution)/shard_map/reduce_scatter | solution.py:153
  609.7 437.4 %all-reduce.4.cloned.1.call-start = ((), (), s32[]{:S(2)}) async-start(), calls=%async_computation.11 | async-start | bytes 4194304 | tf_op jit(solution)/shard_map/psum | solution.py:165
  611.8 220.3 %copy-start.5 = (bf16[8192,128]{1,0:T(8,128)(2,1)S(1)}, bf16[8192,128]{1,0:T(8,128)(2,1)}, u32[]{:S(2)}) copy-start(bf16[8192,128]{1,0:T(8,128)(2,1)} %all-gather.17.cloned.1.call-done) | copy-start | bytes 6291460
  947.0 100.1 %copy-start.4 = (bf16[2,64,8192]{2,1,0:T(8,128)(2,1)S(1)}, bf16[2,64,8192]{2,1,0:T(8,128)(2,1)}, u32[]{:S(2)}) copy-start(bf16[2,64,8192]{2,1,0:T(8,128)(2,1)} %all-gather.11.cloned.1.call-done) | copy-start | bytes 6291460
  952.0 168.4 %all-gather.23.cloned.1.call-start = ((), (), s32[]{:S(2)}) async-start(), calls=%async_computation.12 | async-start | bytes 2162688 | tf_op jit(solution)/shard_map/all_gather | solution.py:176
  955.1 94.3 %copy-start.7 = (bf16[2,64,1024]{2,1,0:T(8,128)(2,1)S(1)}, bf16[2,64,1024]{2,1,0:T(8,128)(2,1)}, u32[]{:S(2)}) copy-start(bf16[2,64,1024]{2,1,0:T(8,128)(2,1)} %select_select_fusion) | copy-start | bytes 786436
  1053.6 70.1 %copy-start.1 = (bf16[2,64,512]{2,1,0:T(8,128)(2,1)S(1)}, bf16[2,64,512]{2,1,0:T(8,128)(2,1)}, u32[]{:S(2)}) copy-start(bf16[2,64,512]{2,1,0:T(8,128)(2,1)} %param.23) | copy-start | bytes 393220
Sparse Core Ops, SparseCore 0:
  45.8 83.3 reduce-scatter.2
  131.8 66.0 all-gather.8
  201.8 57.9 all-gather.10
  261.6 63.3 all-gather.16
  326.9 64.3 all-gather.12
  393.2 72.0 all-gather.20
  467.9 63.4 all-gather.18
  534.0 63.3 all-gather.14
  605.1 226.1 all-reduce.5
  833.6 113.2 reduce-scatter.4
  952.2 94.8 all-reduce.3
  1051.9 68.5 all-gather.22
where the time goes:
time: 1130 us
  waiting for transfers between devices  996 us (88%)
  matrix products  50.7 us (4%)
  blocking collectives  30 us (3%)
  local copies, waits for them, and re-layouts  20.6 us (2%)
  other arithmetic  17.4 us (2%)
  between operations  15.3 us (1%)
    unnamed x13, waiting for transfers between devices  213 us
    reduce_scatter x1, waiting for transfers between devices, per_device(): lax.psum_scatter(value_term.astype(jnp.bfloat16), 'sec', scatter_dimensio...  110 us
    psum x1, waiting for transfers between devices, per_device(): lax.psum(grad_part.astype(jnp.bfloat16), 'tp').astype(jnp.float32)  91.9 us
    reduce_scatter x1, waiting for transfers between devices, per_device(): lax.psum_scatter(partial_value, 'tp', scatter_dimension=1, tiled=True)  83.5 us
    all_gather x1, waiting for transfers between devices, per_device(): lax.all_gather(query_weight, 'sec', axis=0, tiled=True)  70.6 us
    all_gather x1, waiting for transfers between devices, per_device(): lax.all_gather(value_weight, 'sec', axis=0, tiled=True)  63.3 us
    all_gather x1, waiting for transfers between devices, per_device(): lax.all_gather(compact_grads, 'sec', axis=0, tiled=True)  62.6 us
    all_gather x1, waiting for transfers between devices, per_device(): lax.all_gather(keys_mine, 'sec', axis=1, tiled=True)  61.4 us
  transfers between devices with their start and end apart: 12, of which 12 were waited for; matrix products, arithmetic and copies ran while one was open for 5% of the time, Pallas kernels for 0%

commit v1 on v0

v1 whole, which is shorter than its diff:
```python
import functools
import math

import jax
import jax.numpy as jnp
from jax import lax
from jax.experimental import pallas as pl
from jax.experimental.pallas import tpu as pltpu
from jax.sharding import PartitionSpec as P

HEAD_DIM = 128
BF = jnp.bfloat16
F32 = jnp.float32
MESH = pl.DeviceIdType.MESH


def dot_nn(a, b):
    return jnp.dot(a, b, preferred_element_type=F32)


def dot_nt(a, b):
    return lax.dot_general(a, b, (((1,), (1,)), ((), ())), preferred_element_type=F32)


def dot_tn(a, b):
    return lax.dot_general(a, b, (((0,), (0,)), ((), ())), preferred_element_type=F32)


def row_tile(column):
    return jnp.broadcast_to(column, (128, 128)).T[:8]


def column_of(tile):
    return jnp.broadcast_to(tile[0:1, :], (128, 128)).T


def kernel(nz, nt, ny, names, *refs):
    r = dict(zip(names, refs))
    patches, gain, bias, inner, outer = (r[n] for n in ("patches", "gain", "bias", "inner", "outer"))
    text, w, cot = r["text"], r["w"], r["cot"]
    ssem, rsem, lsem = r["ssem"], r["rsem"], r["lsem"]
    sec, t = lax.axis_index("sec"), lax.axis_index("tp")
    z, s4 = lax.div(sec, 4), lax.rem(sec, 4)
    xl, c = lax.div(s4, 2), lax.rem(s4, 2)
    nxh = nt // ny
    xh, y = lax.div(t, ny), lax.rem(t, ny)
    rows, pw = patches.shape
    chunk = text.shape[2] // 4
    plane = 4 * 128
    images = 4 * rows
    width = text.shape[2] * nt
    seq = nz * 256
    scale = 1.0 / math.sqrt(HEAD_DIM)

    def zmod(v):
        return lax.rem(v + nz, nz)

    def to_t(d):
        dx, dy = d // ny, d % ny
        return lax.rem(xh + dx, nxh) * ny + lax.rem(y + dy, ny)

    def from_t(d):
        dx, dy = d // ny, d % ny
        return lax.rem(xh + nxh - dx, nxh) * ny + lax.rem(y + ny - dy, ny)

    def near(k):
        a = 1 - xl if k // 2 else xl
        b = 1 - c if k % 2 else c
        return a, b

    def dev(zz, xx, cc, tt):
        return (zz * 4 + xx * 2 + cc, tt)

    counter = [0]
    pending = []

    def alloc(n):
        first = counter[0]
        counter[0] += n
        assert counter[0] <= r["n_sem"]
        return first

    def rcopy(src, dst, k, to):
        return pltpu.make_async_remote_copy(
            src_ref=src, dst_ref=dst, send_sem=ssem.at[k], recv_sem=rsem.at[k], device_id=to, device_id_type=MESH
        )

    right, left = dev(zmod(z + 1), xl, c, t), dev(zmod(z - 1), xl, c, t)
    cross = dev(z, 1 - xl, c, t)
    twin = dev(z, xl, 1 - c, t)

    def send(src, dst, k, to):
        copy = rcopy(src, dst, k, to)
        copy.start()
        pending.append(copy)

    def recv(dst, k):
        rcopy(dst, dst, k, twin).wait_recv()

    locals_ = [0]

    def lcopy(src, dst):
        copy = pltpu.make_async_copy(src, dst, lsem.at[locals_[0]])
        locals_[0] += 1
        copy.start()
        return copy

    n_right, n_left = nz // 2, (nz - 1) // 2

    class Ring:
        def __init__(self, slot):
            self.slot = slot
            self.kr, self.kl = alloc(n_right), alloc(n_left)

        def start(self):
            mine = self.slot(z)
            send(mine, mine, self.kr, right)
            if n_left:
                send(mine, mine, self.kl, left)

        def step(self, i):
            came = []
            ref = self.slot(zmod(z - i))
            recv(ref, self.kr + i - 1)
            came.append(zmod(z - i))
            if i < n_right:
                send(ref, ref, self.kr + i, right)
            if i <= n_left:
                ref = self.slot(zmod(z + i))
                recv(ref, self.kl + i - 1)
                came.append(zmod(z + i))
                if i < n_left:
                    send(ref, ref, self.kl + i, left)
            return came

    inner_copy = lcopy(inner, r["inner_v"])
    outer_copies = [
        lcopy(outer.at[:, pl.ds(pl.multiple_of((tt * 4 + s4) * chunk, chunk), chunk)], r["outer_v"].at[tt])
        for tt in range(nt)
    ]

    barrier = pltpu.get_barrier_semaphore()
    peers = [dev(z, xl, c, to_t(d)) for d in range(1, nt)]
    peers += [dev(z, *near(k), t) for k in range(1, 4)] + [right, left]
    for peer in peers:
        pl.semaphore_signal(barrier, inc=1, device_id=peer, device_id_type=MESH)
    pl.semaphore_wait(barrier, len(peers))

    pall, a_ref, wg, d_out = r["pall"], r["a"], r["wg"], r["d_out"]
    k_patch = alloc(nt)
    for d in range(1, nt):
        send(patches, pall.at[t], k_patch + d, dev(z, xl, c, to_t(d)))
    k_text = alloc(4)
    for k in range(1, 4):
        xx, cc = near(k)
        part = text.at[:, :, pl.ds(pl.multiple_of((xx * 2 + cc) * chunk, chunk), chunk)]
        send(part, a_ref.at[t, pl.ds(2 * xl, 2), c], k_text + k, dev(z, xx, cc, t))
    w_own = wg.at[pl.ds(pl.multiple_of(z * 256, 256), 256)]
    own_copies = [
        lcopy(patches, pall.at[t]),
        lcopy(
            text.at[:, :, pl.ds(pl.multiple_of(s4 * chunk, chunk), chunk)], a_ref.at[t, pl.ds(2 * xl, 2), c]
        ),
        lcopy(w, w_own),
        lcopy(cot.at[c], d_out.at[c]),
    ]
    k_cot = alloc(1)
    send(cot.at[1 - c], d_out.at[c], k_cot, twin)
    for copy in own_copies:
        copy.wait()
    ring_w = Ring(lambda zz: wg.at[pl.ds(pl.multiple_of(zz * 256, 256), 256)])
    ring_w.start()

    pick, place, mask = r["pick"], r["place"], r["mask"]
    total = nz * images
    pick[...] = jnp.where(
        r["grow"][...] == z * images + lax.broadcasted_iota(jnp.int32, (images, total), 0), 1.0, 0.0
    ).astype(BF)
    stands = jnp.where(
        r["krow"][...] == z * plane + lax.broadcasted_iota(jnp.int32, (plane, total), 0), 1.0, 0.0
    ).astype(BF)
    place[...] = dot_nt(stands, pick[...]).astype(BF)
    mask[...] = dot_nn(place[...], jnp.ones((images, chunk), BF))

    for k in range(1, 4):
        xx, cc = near(k)
        recv(a_ref.at[t, pl.ds(2 * xx, 2), cc], k_text + k)
    k_a = alloc(nt)
    for d in range(1, nt):
        send(a_ref.at[t], a_ref.at[t], k_a + d, dev(z, xl, c, to_t(d)))

    for d in range(1, nt):
        recv(pall.at[from_t(d)], k_patch + d)
    inner_copy.wait()
    vit = gain.shape[1]
    per = vit // pw
    hidden = None
    for piece in range(nt // per):
        wide = jnp.concatenate([pall[piece * per + i] for i in range(per)], axis=1).astype(F32)
        centre = jnp.mean(wide, axis=1, keepdims=True)
        shifted = wide - centre
        spread = jnp.mean(shifted * shifted, axis=1, keepdims=True)
        normed = (shifted * lax.rsqrt(spread + 1e-06) * gain[...] + bias[...]).astype(BF)
        term = dot_nn(normed, r["inner_v"][piece * vit : (piece + 1) * vit, :])
        hidden = term if hidden is None else hidden + term
    hidden = (0.5 * hidden * (1.0 + lax.erf(hidden * math.sqrt(0.5)))).astype(BF)

    def gather_sec(buf, own_value, n, extra=None):
        def block(zz, cc):
            return buf.at[cc, :, pl.ds(pl.multiple_of(zz * n, n), n), :]

        def half(xx):
            return buf.at[c, xx, pl.ds(pl.multiple_of(z * n, n), n), :]

        buf[c, xl, pl.ds(pl.multiple_of(z * n, n), n), :] = own_value
        k_cross, k_twin = alloc(1), alloc(nz)
        send(half(xl), half(xl), k_cross, cross)
        recv(half(1 - xl), k_cross)
        ring = Ring(lambda zz: block(zz, c))
        ring.start()
        send(block(z, c), block(z, c), k_twin, twin)
        done = [z]
        for i in range(1, n_right + 1):
            for zz in ring.step(i):
                send(block(zz, c), block(zz, c), k_twin + len(done), twin)
                done.append(zz)
            if extra is not None:
                extra(i)
        for j, zz in enumerate(done):
            recv(block(zz, 1 - c), k_twin + j)

    hall = r["hall"]
    if n_right > 1:
        ring_w.step(1)
    gather_sec(hall, hidden, rows)
    if n_right > 2:
        ring_w.step(2)

    hp = dot_nn(pick[...], hall[...].reshape(total, hall.shape[3])).astype(BF)
    for copy in outer_copies:
        copy.wait()
    part_s, part_r, img = r["part_s"], r["part_r"], r["img"]
    k_part, k_img = alloc(nt), alloc(nt)
    for d in range(1, nt):
        part_s[d] = dot_nn(hp, r["outer_v"][to_t(d)]).astype(BF)
        send(part_s.at[d], part_r.at[d], k_part + d, dev(z, xl, c, to_t(d)))
    mine = dot_nn(hp, r["outer_v"][t])
    for d in range(1, nt):
        recv(part_r.at[d], k_part + d)
        mine = mine + part_r[d].astype(F32)
    img[t] = mine.astype(BF)
    for d in range(1, nt):
        send(img.at[t], img.at[t], k_img + d, dev(z, xl, c, to_t(d)))
    if n_right > 3:
        ring_w.step(3)

    xf, ss = r["xf"], r["ss"]

    def take(tt):
        placed = dot_nn(place[...], img[tt])
        x = jnp.where(mask[...] > 0.5, placed, a_ref[tt].reshape(plane, chunk).astype(F32))
        xf[:, pl.ds(pl.multiple_of(tt * chunk, chunk), chunk)] = x.astype(BF)
        x = x * x
        return x[:, :128] + x[:, 128:]

    ss[...] = take(t)

    def take_next(d, carry):
        recv(a_ref.at[from_t(d)], k_a + d)
        recv(img.at[from_t(d)], k_img + d)
        ss[...] += take(from_t(d))
        return carry

    lax.fori_loop(1, nt, take_next, 0)
    ss_all, inv = r["ss_all"], r["inv"]
    squares = jnp.sum(ss[...], axis=1, keepdims=True)
    for o in range(4):
        ss_all[s4, o] = row_tile(squares[o * 128 : (o + 1) * 128])
    k_ss, k_c = alloc(4), alloc(4)
    for k in range(1, 4):
        send(ss_all.at[s4], ss_all.at[s4], k_ss + k, dev(z, *near(k), t))
    ring_w.step(n_right)

    c_s, c_r, cn = r["c_s"], r["c_r"], r["cn"]
    for k in (3, 2, 1, 0):
        xx, cc = near(k)
        o = xx * 2 + cc
        c_o = dot_nn(xf[pl.ds(pl.multiple_of(o * 128, 128), 128), :], wg[...])
        if k:
            c_s[k] = c_o.astype(BF)
            send(c_s.at[k], c_r.at[k], k_c + k, dev(z, xx, cc, t))
        else:
            cn[...] = c_o
    for k in range(1, 4):
        xx, cc = near(k)
        recv(ss_all.at[xx * 2 + cc], k_ss + k)
    for o in range(4):
        tile = ss_all[0, o] + ss_all[1, o] + ss_all[2, o] + ss_all[3, o]
        inv[o] = column_of(lax.rsqrt(tile / width + 1e-06))
    projected = cn[...]
    for k in range(1, 4):
        recv(c_r.at[k], k_c + k)
        projected = projected + c_r[k].astype(F32)
    projected = projected * inv[s4][:, :1]
    cn[...] = projected
    heads = (projected.shape[1] - 2 * HEAD_DIM) // HEAD_DIM
    qs, kv, dos = r["qs"], r["kv"], r["dos"]
    for h in range(heads):
        qs[h] = projected[:, h * 128 : (h + 1) * 128].astype(BF)
    kv[z, xl] = projected[:, heads * 128 :].astype(BF)

    k_kv = alloc(1)
    send(kv.at[z, xl], kv.at[z, xl], k_kv, cross)
    recv(kv.at[z, 1 - xl], k_kv)
    ring_kv = Ring(lambda zz: kv.at[zz])
    ring_kv.start()
    recv(d_out.at[1 - c], k_cot)
    for h in range(heads):
        dos[h] = d_out[:, :, h * 128 : (h + 1) * 128].reshape(128, 128)
    for i in range(1, n_right + 1):
        ring_kv.step(i)

    ph, ds, att, dq = r["ph"], r["ds"], r["att"], r["dq"]

    def head(h, carry):
        keys = kv[:, :, :, :128].reshape(seq, 128)
        values = kv[:, :, :, 128:].reshape(seq, 128)
        scores = dot_nt(qs[h], keys) * scale
        query_pos = z * 256 + xl * 128 + lax.broadcasted_iota(jnp.int32, (128, seq), 0)
        scores = jnp.where(lax.broadcasted_iota(jnp.int32, (128, seq), 1) <= query_pos, scores, -1e30)
        raw = jnp.exp(scores - jnp.max(scores, axis=1, keepdims=True))
        probs = raw / jnp.sum(raw, axis=1, keepdims=True)
        half = probs.astype(BF)
        ph[h] = half
        att[h] = dot_nn(half, values).astype(BF)
        grad_probs = dot_nt(dos[h], values)
        delta = jnp.sum(probs * grad_probs, axis=1, keepdims=True)
        grad = (probs * (grad_probs - delta)).astype(BF)
        ds[h] = grad
        dq[h] = (dot_nn(grad, keys) * scale).astype(BF)
        return carry

    lax.fori_loop(0, heads, head, 0)
    att_o, att_r = r["att_o"], r["att_r"]
    for h in range(heads):
        att_o[:, :, h * 128 : (h + 1) * 128] = att[h].reshape(2, 64, 128)
    k_att = alloc(1)
    send(att_o.at[1 - c], att_r, k_att, twin)

    dkv = r["dkv"]

    def key_block(zz, carry):
        lanes = pl.ds(pl.multiple_of(zz * 256, 256), 256)
        dkv[zz, :, :128] = dot_tn(ds[:, :, lanes].reshape(heads * 128, 256), qs[...].reshape(heads * 128, 128))
        dkv[zz, :, 128:] = dot_tn(ph[:, :, lanes].reshape(heads * 128, 256), dos[...].reshape(heads * 128, 128))
        return carry

    lax.fori_loop(0, nz, key_block, 0)

    sr, rr, sl, rl = r["sr"], r["rr"], r["sl"], r["rl"]
    kr, kl = alloc(n_right), alloc(max(n_left, 1))
    for i in range(n_right + 1):
        value = dkv[zmod(z + n_right - i)]
        if i:
            recv(rr.at[i - 1], kr + i - 1)
            value = value + rr[i - 1].astype(F32)
        if i < n_right:
            sr[i] = value.astype(BF)
            send(sr.at[i], rr.at[i], kr + i, right)
        else:
            dkv[z] = value
        if n_left and i < n_left:
            value = dkv[zmod(z - n_left + i)]
            if i:
                recv(rl.at[i - 1], kl + i - 1)
                value = value + rl[i - 1].astype(F32)
            sl[i] = value.astype(BF)
            send(sl.at[i], rl.at[i], kl + i, left)
    if n_left:
        recv(rl.at[n_left - 1], kl + n_left - 1)
        dkv[z] += rl[n_left - 1].astype(F32)
    dx_s, dx_r = r["dx_s"], r["dx_r"]
    k_dx = alloc(1)
    dx_s[...] = dkv[z, pl.ds(pl.multiple_of((1 - xl) * 128, 128), 128), :].astype(BF)
    send(dx_s, dx_r, k_dx, cross)
    recv(dx_r, k_dx)
    grad_kv = dkv[z, pl.ds(pl.multiple_of(xl * 128, 128), 128), :] + dx_r[...].astype(F32)

    gg, inn, int_all = r["gg"], r["inn"], r["int_all"]
    pieces = [dq[h] for h in range(heads)]
    pieces += [(grad_kv[:, :128] * scale).astype(BF), grad_kv[:, 128:].astype(BF)]
    grads = jnp.concatenate(pieces, axis=1)
    gg[s4] = grads
    inn[s4] = row_tile(jnp.sum(grads.astype(F32) * cn[...], axis=1, keepdims=True))
    k_gg, k_inn = alloc(4), alloc(4)
    for k in range(1, 4):
        to = dev(z, *near(k), t)
        send(gg.at[s4], gg.at[s4], k_gg + k, to)
        send(inn.at[s4], inn.at[s4], k_inn + k, to)
    for k in range(1, 4):
        xx, cc = near(k)
        recv(gg.at[xx * 2 + cc], k_gg + k)
        recv(inn.at[xx * 2 + cc], k_inn + k)
    int_all[t] = inn[...]
    k_int, k_back = alloc(nt), alloc(nt)
    for d in range(1, nt):
        send(int_all.at[t], int_all.at[t], k_int + d, dev(z, xl, c, to_t(d)))

    bs, br, bo = r["bs"], r["br"], r["bo"]

    def back(d, carry):
        tt = to_t(d)
        block = dot_nt(
            gg[...].reshape(plane, gg.shape[2]), wg[pl.ds(pl.multiple_of(tt * chunk, chunk), chunk), :]
        )
        bs[d] = block.astype(BF)
        rcopy(bs.at[d], br.at[d], k_back + d, dev(z, xl, c, tt)).start()
        return carry

    lax.fori_loop(1, nt, back, 0)
    for d in range(1, nt):
        pending.append(rcopy(bs.at[d], br.at[d], k_back + d, dev(z, xl, c, to_t(d))))
    bo[...] = dot_nt(gg[...].reshape(plane, gg.shape[2]), wg[pl.ds(pl.multiple_of(t * chunk, chunk), chunk), :])
    for d in range(1, nt):
        recv(int_all.at[from_t(d)], k_int + d)
    for d in range(1, nt):
        recv(br.at[d], k_back + d)
        bo[...] += br[d].astype(F32)
    gi, gt_s, gt_r = r["gi"], r["gt_s"], r["gt_r"]
    for o in range(4):
        tile = int_all[0, o]
        for d in range(1, nt):
            tile = tile + int_all[d, o]
        inv_o = inv[o][:, :1]
        span = slice(o * 128, (o + 1) * 128)
        x = xf[span, pl.ds(pl.multiple_of(t * chunk, chunk), chunk)].astype(F32)
        grad = (inv_o * bo[span, :] - x * (inv_o * inv_o * column_of(tile)[:, :1] / width)).astype(BF)
        gi[span, :] = grad
        gt_s[o] = jnp.where(mask[span, :] > 0.5, jnp.zeros_like(grad), grad).reshape(2, 64, chunk)

    k_gt = alloc(4)
    for k in range(1, 4):
        xx, cc = near(k)
        send(gt_s.at[pl.ds(2 * xx, 2), cc], gt_r.at[s4], k_gt + k, dev(z, xx, cc, t))
    rall = r["rall"]
    gather_sec(rall, dot_tn(place[...], gi[...]).astype(BF), images)
    wanted = jnp.where(r["gcol"][...] == lax.broadcasted_iota(jnp.int32, (rows, total), 1), 1.0, 0.0).astype(BF)
    for xx in range(2):
        for cc in range(2):
            o = xx * 2 + cc
            r["gimage"][:, o * chunk : (o + 1) * chunk] = dot_nn(wanted, rall[cc, xx]).astype(BF)

    gt_r[s4] = gt_s[pl.ds(2 * xl, 2), c]
    for k in range(1, 4):
        xx, cc = near(k)
        recv(gt_r.at[xx * 2 + cc], k_gt + k)
    for o in range(4):
        r["gtext"][:, :, o * chunk : (o + 1) * chunk] = gt_r[o]
    recv(att_r, k_att)
    r["attended"][c] = att_o[c]
    r["attended"][1 - c] = att_r[...]
    for copy in pending:
        copy.wait_send()


def per_device(
    patches,
    merge_gain,
    merge_bias,
    merge_inner,
    merge_outer,
    slot_target,
    text_embed,
    norm_gain,
    query_weight,
    key_weight,
    value_weight,
    attn_cotangent,
):
    nsec, nt = lax.axis_size("sec"), lax.axis_size("tp")
    nz, ny = nsec // 4, max(nt // 2, 1)
    sec = lax.axis_index("sec")
    rows, pw = patches.shape
    hid = merge_inner.shape[1]
    micro, tok, feat = text_embed.shape
    chunk = feat // 4
    seq = tok * nsec
    images = 4 * rows
    total = nz * images
    depth = query_weight.shape[0]
    heads = query_weight.shape[1] // HEAD_DIM
    cols = (heads + 2) * HEAD_DIM
    plane = 512

    batch, pos = slot_target // seq, slot_target % seq
    key = (pos // 256) * plane + (pos // 128 % 2) * 256 + batch * 128 + pos % 128
    rank = jnp.sum((key[None, :] < key[:, None]).astype(jnp.int32), axis=1)

    def row_order(v):
        return v.reshape(nz, 2, 2, rows).transpose(2, 1, 0, 3).reshape(1, total)

    gcol = lax.dynamic_slice_in_dim(rank, sec * rows, rows).reshape(rows, 1)
    my_gain = lax.dynamic_slice_in_dim(norm_gain, sec * depth, depth)[:, None]
    weight = jnp.concatenate([query_weight, key_weight, value_weight], axis=1)
    weight = (weight.astype(F32) * my_gain).astype(BF)

    vmem, anyspace = pl.BlockSpec(memory_space=pltpu.VMEM), pl.BlockSpec(memory_space=pl.ANY)
    n_right, n_left = nz // 2, max((nz - 1) // 2, 1)
    n_sem = 192
    ins = ["patches", "gain", "bias", "inner", "outer", "krow", "grow", "gcol", "text", "w", "cot"]
    outs = ["attended", "gtext", "gimage"]
    scratch = dict(
        pall=((nt, rows, pw), BF),
        inner_v=(merge_inner.shape, BF),
        outer_v=((nt, hid, chunk), BF),
        a=((nt, 4, 2, tok, chunk), BF),
        wg=((nz * depth, cols), BF),
        d_out=((2, tok, heads * HEAD_DIM), BF),
        hall=((2, 2, nz * rows, hid), BF),
        pick=((images, total), BF),
        place=((plane, images), BF),
        mask=((plane, chunk), F32),
        part_s=((nt, images, chunk), BF),
        part_r=((nt, images, chunk), BF),
        img=((nt, images, chunk), BF),
        xf=((plane, nt * chunk), BF),
        ss=((plane, 128), F32),
        ss_all=((4, 4, 8, 128), F32),
        inv=((4, 128, 128), F32),
        c_s=((4, 128, cols), BF),
        c_r=((4, 128, cols), BF),
        cn=((128, cols), F32),
        qs=((heads, 128, 128), BF),
        kv=((nz, 2, 128, 256), BF),
        dos=((heads, 128, 128), BF),
        ph=((heads, 128, seq), BF),
        ds=((heads, 128, seq), BF),
        att=((heads, 128, 128), BF),
        dq=((heads, 128, 128), BF),
        att_o=((2, tok, heads * HEAD_DIM), BF),
        att_r=((tok, heads * HEAD_DIM), BF),
        dkv=((nz, 256, 256), F32),
        sr=((n_right, 256, 256), BF),
        rr=((n_right, 256, 256), BF),
        sl=((n_left, 256, 256), BF),
        rl=((n_left, 256, 256), BF),
        dx_s=((128, 256), BF),
        dx_r=((128, 256), BF),
        gg=((4, 128, cols), BF),
        inn=((4, 8, 128), F32),
        int_all=((nt, 4, 8, 128), F32),
        bs=((nt, plane, chunk), BF),
        br=((nt, plane, chunk), BF),
        bo=((plane, chunk), F32),
        gi=((plane, chunk), BF),
        gt_s=((4, 2, tok, chunk), BF),
        gt_r=((4, 2, tok, chunk), BF),
        rall=((2, 2, nz * images, chunk), BF),
    )
    names = ins + outs + list(scratch) + ["ssem", "rsem", "lsem", "n_sem"]
    call = pl.pallas_call(
        lambda *refs: kernel(nz, nt, ny, names, *refs, n_sem),
        out_shape=(
            jax.ShapeDtypeStruct((micro, tok, heads * HEAD_DIM), BF),
            jax.ShapeDtypeStruct((micro, tok, feat), BF),
            jax.ShapeDtypeStruct((rows, feat), BF),
        ),
        in_specs=[anyspace if n in ("inner", "outer") else vmem for n in ins],
        out_specs=(vmem,) * 3,
        scratch_shapes=[pltpu.VMEM(shape, dtype) for shape, dtype in scratch.values()]
        + [
            pltpu.SemaphoreType.DMA((n_sem,)),
            pltpu.SemaphoreType.DMA((n_sem,)),
            pltpu.SemaphoreType.DMA((16,)),
        ],
        compiler_params=pltpu.CompilerParams(
            collective_id=0, has_side_effects=True, vmem_limit_bytes=56 * 1024 * 1024
        ),
        name="merged_step",
    )
    return call(
        patches,
        merge_gain.reshape(1, -1),
        merge_bias.reshape(1, -1),
        merge_inner,
        merge_outer,
        row_order(key),
        row_order(rank),
        gcol,
        text_embed,
        weight,
        attn_cotangent,
    )


def solution(mesh):
    return jax.shard_map(
        per_device,
        mesh=mesh,
        in_specs=(
            P("sec", "tp"),
            P(),
            P(),
            P(None, "tp"),
            P("tp", None),
            P(),
            P(None, "sec", "tp"),
            P(),
            P("sec", "tp"),
            P("sec", "tp"),
            P("sec", "tp"),
            P(None, "sec", "tp"),
        ),
        out_specs=(P(None, "sec", "tp"), P(None, "sec", "tp"), P("sec", "tp")),
        check_vma=False,
    )
```

time: 1130 us -> 224 us (0.20)
  waiting for transfers between devices: 996 us -> 0 us
  Pallas kernels: 0 us -> 207 us
  matrix products: 50.7 us -> 0 us
  blocking collectives: 30 us -> 0 us
  between operations: 15.3 us -> 0.67 us
  other arithmetic: 17.4 us -> 3.17 us
    all_gather x8 -> x0, waiting for transfers between devices: 497 us -> none  [the longest x1 70.6 us: per_device(): lax.all_gather(query_weight, 'sec', axis=0, tiled=True)]
    unnamed x13 -> x0, waiting for transfers between devices: 213 us -> none
    pallas_call x0 -> x1, Pallas kernels: none -> 207 us  [per_device(): call(patches, merge_gain.reshape(1, -1), merge_bias.reshape(1, -1), merge...]
    reduce_scatter x2 -> x0, waiting for transfers between devices: 194 us -> none  [the longest x1 110 us: per_device(): lax.psum_scatter(value_term.astype(jnp.bfloat16), 'sec', scatter_dimensio...]
    psum x1 -> x0, waiting for transfers between devices: 91.9 us -> none  [per_device(): lax.psum(grad_part.astype(jnp.bfloat16), 'tp').astype(jnp.float32)]
    dot_general x13 -> x0, matrix products: 50.7 us -> none  [the longest x1 8.28 us: per_device(): jnp.dot(grad_q, query_full.T, preferred_element_type=jnp.float32)]
    all_gather x1 -> x0, blocking collectives: 30 us -> none  [per_device(): full_rows = lax.all_gather(patches, 'tp', axis=1, tiled=True)]
  transfers between devices with their start and end apart: 12 -> 0, of which waited for: 12 -> 0; matrix products, arithmetic and copies ran while one was open for 5% -> 0% of each run, Pallas kernels for 0% -> 0%
where the time goes in v1:
time: 224 us; the launch traced here: 221 us
  Pallas kernels  207 us (92%)
  local copies, waits for them, and re-layouts  10.3 us (5%)
  other arithmetic  3.17 us (1%)
    pallas_call x1, Pallas kernels, per_device(): call(patches, merge_gain.reshape(1, -1), merge_bias.reshape(1, -1), merge...  207 us
    unnamed x3, local copies, waits for them, and re-layouts  4.71 us

profile of v1, /device:TPU:1, one launch (start us, length us, event | category | flops | bytes accessed | tf_op | source)
XLA Modules:
  0.0 221.4 jit_solution(16220013821287194392)
XLA Ops:
  0.6 0.8 dynamic_slice.7
  1.4 0.7 fusion.4
  2.1 0.6 convert_reduce_fusion
  2.7 0.1 dynamic-slice_bitcast_fusion
  2.8 1.3 reshape.30.refs_1_
  4.0 1.3 reshape.31.refs_2_
  5.3 0.1 reshape.34
  5.4 0.7 reshape.35.refs_6_
  6.1 0.1 reshape.32
  6.2 0.7 reshape.33.refs_5_
  6.9 0.7 copy.21.refs_7_
  7.6 1.9 multiply_convert_fusion.refs_9_
  9.5 207.3 %merged_step.1 = (bf16[2,64,512]{2,1,0:T(8,128)(2,1)}, bf16[2,64,1024]{2,1,0:T(8,128)(2,1)}, bf16[32,1024]{1,0:T(8,128)(2,1)}) custom-call(bf16[32,640]{1,0:T(8,128)(2,1)} %refs_0_.1, f32[1,1280]{1,0:T(1,128)} %reshape.30.refs_1_, f32[1,1280]{1,0:T(1,128)} %reshape.31.refs_2_, bf16[5120,384]{1,0:T(8,128)(2,1)} %refs_3_.1, bf16[384,8192]{1,0:T(8,128)(2,1)} %refs_4_.1, ...), custom_call_target="tpu_custom_call" | custom-call | tf_op jit(solution)/shard_map/merged_step/pallas_call | solution.py:581
  216.7 1.6 copy.25
  218.3 1.7 copy.26
  220.0 1.5 copy.27
  (2 shorter events, 0.0 us)

commit v2 on v1

--- a/solution.py
+++ b/solution.py
@@ -12,6 +12,8 @@
 BF = jnp.bfloat16
 F32 = jnp.float32
 MESH = pl.DeviceIdType.MESH
+TEXT_AT = 2
+W_AT = 2
 
 
 def dot_nn(a, b):
@@ -37,7 +39,7 @@
 def kernel(nz, nt, ny, names, *refs):
     r = dict(zip(names, refs))
     patches, gain, bias, inner, outer = (r[n] for n in ("patches", "gain", "bias", "inner", "outer"))
-    text, w, cot = r["text"], r["w"], r["cot"]
+    text, cot = r["text"], r["cot"]
     ssem, rsem, lsem = r["ssem"], r["rsem"], r["lsem"]
     sec, t = lax.axis_index("sec"), lax.axis_index("tp")
     z, s4 = lax.div(sec, 4), lax.rem(sec, 4)
@@ -133,6 +135,20 @@
                     send(ref, ref, self.kl + i, left)
             return came
 
+    pall, a_ref, wg, d_out, w_v = r["pall"], r["a"], r["wg"], r["d_out"], r["w_v"]
+    own_copies = [
+        lcopy(patches, pall.at[t]),
+        lcopy(
+            text.at[:, :, pl.ds(pl.multiple_of(s4 * chunk, chunk), chunk)], a_ref.at[t, pl.ds(2 * xl, 2), c]
+        ),
+        lcopy(cot.at[c], d_out.at[c]),
+    ]
+    w_copies = []
+    first = 0
+    for name in ("wq", "wk", "wv"):
+        n = r[name].shape[1]
+        w_copies.append(lcopy(r[name], w_v.at[:, pl.ds(first, n)]))
+        first += n
     inner_copy = lcopy(inner, r["inner_v"])
     outer_copies = [
         lcopy(outer.at[:, pl.ds(pl.multiple_of((tt * 4 + s4) * chunk, chunk), chunk)], r["outer_v"].at[tt])
@@ -146,7 +162,6 @@
         pl.semaphore_signal(barrier, inc=1, device_id=peer, device_id_type=MESH)
     pl.semaphore_wait(barrier, len(peers))
 
-    pall, a_ref, wg, d_out = r["pall"], r["a"], r["wg"], r["d_out"]
     k_patch = alloc(nt)
     for d in range(1, nt):
         send(patches, pall.at[t], k_patch + d, dev(z, xl, c, to_t(d)))
@@ -155,44 +170,77 @@
         xx, cc = near(k)
         part = text.at[:, :, pl.ds(pl.multiple_of((xx * 2 + cc) * chunk, chunk), chunk)]
         send(part, a_ref.at[t, pl.ds(2 * xl, 2), c], k_text + k, dev(z, xx, cc, t))
-    w_own = wg.at[pl.ds(pl.multiple_of(z * 256, 256), 256)]
-    own_copies = [
-        lcopy(patches, pall.at[t]),
-        lcopy(
-            text.at[:, :, pl.ds(pl.multiple_of(s4 * chunk, chunk), chunk)], a_ref.at[t, pl.ds(2 * xl, 2), c]
-        ),
-        lcopy(w, w_own),
-        lcopy(cot.at[c], d_out.at[c]),
-    ]
     k_cot = alloc(1)
     send(cot.at[1 - c], d_out.at[c], k_cot, twin)
+
+    r["gain_v"][...] = r["ngain"][...].reshape(r["gain_v"].shape)
+    for copy in w_copies:
+        copy.wait()
+    for i in range(2):
+        factor = column_of(r["gain_v"][pl.ds(sec * 2 + i, 1), :])[:, :1]
+        rows_i = pl.ds(pl.multiple_of(z * 256 + i * 128, 128), 128)
+        wg[rows_i, :] = (w_v[i * 128 : (i + 1) * 128, :].astype(F32) * factor).astype(BF)
+    ring_w = Ring(lambda zz: wg.at[pl.ds(pl.multiple_of(zz * 256, 256), 256)])
+    ring_w.start()
+
+    pick, place, mask, kcol = r["pick"], r["place"], r["mask"], r["kcol"]
+    total = nz * images
+    slot = r["slot"][...].reshape(1, total)
+    bits = seq.bit_length() - 1
+    batch, pos = slot >> bits, slot & (seq - 1)
+    key = ((pos >> 8) * plane + ((pos >> 7) & 1) * 256 + batch * 128 + (pos & 127)).astype(F32)
+    for i in range(total // 128):
+        kcol[i * 128 : (i + 1) * 128, :] = column_of(key[:, i * 128 : (i + 1) * 128])
+    rank = jnp.sum(jnp.where(kcol[...][:, :1] < key, 1.0, 0.0), axis=0, keepdims=True)
+    wide_rows = lax.broadcasted_iota(jnp.int32, (images, total), 0) + z * images
+    pick[...] = jnp.where(rank == wide_rows.astype(F32), 1.0, 0.0).astype(BF)
+    wide_rows = lax.broadcasted_iota(jnp.int32, (plane, total), 0) + z * plane
+    stands = jnp.where(key == wide_rows.astype(F32), 1.0, 0.0).astype(BF)
+    place[...] = dot_nt(stands, pick[...]).astype(BF)
+    mask[...] = dot_nn(place[...], jnp.ones((images, chunk), BF))
+    own_key = kcol[pl.ds(pl.multiple_of(z * images, images), images), :][:, :1]
+    own_rank = jnp.sum(jnp.where(key < own_key, 1.0, 0.0), axis=1, keepdims=True)
+    wanted, tsel, isel = r["wanted"], r["tsel"], r["isel"]
+    wanted[...] = jnp.where(
+        own_rank == lax.broadcasted_iota(jnp.int32, (images, total), 1).astype(F32), 1.0, 0.0
+    ).astype(BF)
+    earlier = jnp.where(
+        lax.broadcasted_iota(jnp.int32, (128, 128), 0) < lax.broadcasted_iota(jnp.int32, (128, 128), 1), 1.0, 0.0
+    ).astype(BF)
+
+    def select(flags, count):
+        nth = dot_nn(flags[:8].astype(BF), earlier)[:1]
+        return jnp.where(
+            nth == lax.broadcasted_iota(jnp.int32, (count, 128), 0).astype(F32), flags[:1], 0.0
+        ).astype(BF)
+
+    texts = 128 - rows
+    for o in range(4):
+        tsel[o] = select(1.0 - mask[o * 128 : (o + 1) * 128, :128].T, texts)
+    isel[...] = select(mask[pl.ds(pl.multiple_of(s4 * 128, 128), 128), :128].T, rows)
+
     for copy in own_copies:
         copy.wait()
-    ring_w = Ring(lambda zz: wg.at[pl.ds(pl.multiple_of(zz * 256, 256), 256)])
-    ring_w.start()
-
-    pick, place, mask = r["pick"], r["place"], r["mask"]
-    total = nz * images
-    pick[...] = jnp.where(
-        r["grow"][...] == z * images + lax.broadcasted_iota(jnp.int32, (images, total), 0), 1.0, 0.0
-    ).astype(BF)
-    stands = jnp.where(
-        r["krow"][...] == z * plane + lax.broadcasted_iota(jnp.int32, (plane, total), 0), 1.0, 0.0
-    ).astype(BF)
-    place[...] = dot_nt(stands, pick[...]).astype(BF)
-    mask[...] = dot_nn(place[...], jnp.ones((images, chunk), BF))
 
     for k in range(1, 4):
         xx, cc = near(k)
         recv(a_ref.at[t, pl.ds(2 * xx, 2), cc], k_text + k)
     k_a = alloc(nt)
-    for d in range(1, nt):
-        send(a_ref.at[t], a_ref.at[t], k_a + d, dev(z, xl, c, to_t(d)))
-
+
+    def text_out():
+        for d in range(1, nt):
+            send(a_ref.at[t], a_ref.at[t], k_a + d, dev(z, xl, c, to_t(d)))
+
+    if TEXT_AT == 0:
+        text_out()
     for d in range(1, nt):
         recv(pall.at[from_t(d)], k_patch + d)
+    if TEXT_AT == 1:
+        text_out()
+    if W_AT == 1:
+        ring_w.step(1)
     inner_copy.wait()
-    vit = gain.shape[1]
+    vit = gain.shape[0]
     per = vit // pw
     hidden = None
     for piece in range(nt // per):
@@ -200,43 +248,58 @@
         centre = jnp.mean(wide, axis=1, keepdims=True)
         shifted = wide - centre
         spread = jnp.mean(shifted * shifted, axis=1, keepdims=True)
-        normed = (shifted * lax.rsqrt(spread + 1e-06) * gain[...] + bias[...]).astype(BF)
+        normed = (shifted * lax.rsqrt(spread + 1e-06) * gain[...].reshape(1, vit) + bias[...].reshape(1, vit)).astype(BF)
         term = dot_nn(normed, r["inner_v"][piece * vit : (piece + 1) * vit, :])
         hidden = term if hidden is None else hidden + term
     hidden = (0.5 * hidden * (1.0 + lax.erf(hidden * math.sqrt(0.5)))).astype(BF)
 
-    def gather_sec(buf, own_value, n, extra=None):
-        def block(zz, cc):
-            return buf.at[cc, :, pl.ds(pl.multiple_of(zz * n, n), n), :]
-
-        def half(xx):
-            return buf.at[c, xx, pl.ds(pl.multiple_of(z * n, n), n), :]
-
-        buf[c, xl, pl.ds(pl.multiple_of(z * n, n), n), :] = own_value
-        k_cross, k_twin = alloc(1), alloc(nz)
-        send(half(xl), half(xl), k_cross, cross)
-        recv(half(1 - xl), k_cross)
-        ring = Ring(lambda zz: block(zz, c))
-        ring.start()
-        send(block(z, c), block(z, c), k_twin, twin)
-        done = [z]
-        for i in range(1, n_right + 1):
-            for zz in ring.step(i):
-                send(block(zz, c), block(zz, c), k_twin + len(done), twin)
-                done.append(zz)
-            if extra is not None:
-                extra(i)
-        for j, zz in enumerate(done):
-            recv(block(zz, 1 - c), k_twin + j)
+    class Gather:
+        def __init__(self, slot_of):
+            self.slot_of = slot_of
+            self.k_cross, self.k_twin = alloc(1), alloc(2 * nz)
+            mine = slot_of(z, xl, c)
+            send(mine, mine, self.k_cross, cross)
+            self.rings = [Ring(lambda zz: slot_of(zz, xl, c)), Ring(lambda zz: slot_of(zz, 1 - xl, c))]
+            self.done = []
+            self.rings[0].start()
+            self.arrived(z, xl)
+
+        def arrived(self, zz, xx):
+            ref = self.slot_of(zz, xx, c)
+            send(ref, ref, self.k_twin + len(self.done), twin)
+            self.done.append((zz, xx))
+
+        def crossed(self):
+            recv(self.slot_of(z, 1 - xl, c), self.k_cross)
+            self.rings[1].start()
+            self.arrived(z, 1 - xl)
+
+        def step(self, i):
+            for ring, xx in zip(self.rings, (xl, 1 - xl)):
+                for zz in ring.step(i):
+                    self.arrived(zz, xx)
+
+        def finish(self):
+            for j, (zz, xx) in enumerate(self.done):
+                recv(self.slot_of(zz, xx, 1 - c), self.k_twin + j)
 
     hall = r["hall"]
-    if n_right > 1:
+    hall[z, xl, c] = hidden
+    if W_AT == 2:
         ring_w.step(1)
-    gather_sec(hall, hidden, rows)
+    gather = Gather(lambda zz, xx, cc: hall.at[zz, xx, cc])
+    gather.crossed()
+    if TEXT_AT == 2:
+        text_out()
+    for i in range(1, n_right + 1):
+        gather.step(i)
+    gather.finish()
     if n_right > 2:
         ring_w.step(2)
-
-    hp = dot_nn(pick[...], hall[...].reshape(total, hall.shape[3])).astype(BF)
+    if TEXT_AT == 3:
+        text_out()
+
+    hp = dot_nn(pick[...], hall[...].reshape(total, hall.shape[4])).astype(BF)
     for copy in outer_copies:
         copy.wait()
     part_s, part_r, img = r["part_s"], r["part_r"], r["img"]
@@ -282,15 +345,18 @@
     ring_w.step(n_right)
 
     c_s, c_r, cn = r["c_s"], r["c_r"], r["cn"]
-    for k in (3, 2, 1, 0):
-        xx, cc = near(k)
-        o = xx * 2 + cc
-        c_o = dot_nn(xf[pl.ds(pl.multiple_of(o * 128, 128), 128), :], wg[...])
-        if k:
-            c_s[k] = c_o.astype(BF)
-            send(c_s.at[k], c_r.at[k], k_c + k, dev(z, xx, cc, t))
-        else:
-            cn[...] = c_o
+    def project(xx, cc):
+        return dot_nn(xf[pl.ds(pl.multiple_of((xx * 2 + cc) * 128, 128), 128), :], wg[...])
+
+    c_s[0] = project(1 - xl, 1 - c).astype(BF)
+    send(c_s.at[0], c_r.at[0], k_c, twin)
+    c_s[1] = project(xl, 1 - c).astype(BF)
+    send(c_s.at[1], c_r.at[1], k_c + 1, twin)
+    other = project(1 - xl, c)
+    recv(c_r.at[0], k_c)
+    c_s[2] = (other + c_r[0].astype(F32)).astype(BF)
+    send(c_s.at[2], c_r.at[2], k_c + 2, cross)
+    cn[...] = project(xl, c)
     for k in range(1, 4):
         xx, cc = near(k)
         recv(ss_all.at[xx * 2 + cc], k_ss + k)
@@ -298,7 +364,7 @@
         tile = ss_all[0, o] + ss_all[1, o] + ss_all[2, o] + ss_all[3, o]
         inv[o] = column_of(lax.rsqrt(tile / width + 1e-06))
     projected = cn[...]
-    for k in range(1, 4):
+    for k in range(1, 3):
         recv(c_r.at[k], k_c + k)
         projected = projected + c_r[k].astype(F32)
     projected = projected * inv[s4][:, :1]
@@ -311,14 +377,22 @@
 
     k_kv = alloc(1)
     send(kv.at[z, xl], kv.at[z, xl], k_kv, cross)
+    rings = [Ring(lambda zz: kv.at[zz, xl]), Ring(lambda zz: kv.at[zz, 1 - xl])]
+    rings[0].start()
     recv(kv.at[z, 1 - xl], k_kv)
-    ring_kv = Ring(lambda zz: kv.at[zz])
-    ring_kv.start()
+    rings[1].start()
+    own_s, own_r = r["own_s"], r["own_r"]
+    k_own = alloc(nt)
+    h_own = hall[z].reshape(images, hall.shape[4])
+    for d in range(1, nt):
+        own_s[d] = dot_nn(h_own, r["outer_v"][to_t(d)]).astype(BF)
+        send(own_s.at[d], own_r.at[d], k_own + d, dev(z, xl, c, to_t(d)))
     recv(d_out.at[1 - c], k_cot)
     for h in range(heads):
         dos[h] = d_out[:, :, h * 128 : (h + 1) * 128].reshape(128, 128)
     for i in range(1, n_right + 1):
-        ring_kv.step(i)
+        rings[0].step(i)
+        rings[1].step(i)
 
     ph, ds, att, dq = r["ph"], r["ds"], r["att"], r["dq"]
 
@@ -358,60 +432,94 @@
     lax.fori_loop(0, nz, key_block, 0)
 
     sr, rr, sl, rl = r["sr"], r["rr"], r["sl"], r["rl"]
-    kr, kl = alloc(n_right), alloc(max(n_left, 1))
-    for i in range(n_right + 1):
-        value = dkv[zmod(z + n_right - i)]
-        if i:
-            recv(rr.at[i - 1], kr + i - 1)
-            value = value + rr[i - 1].astype(F32)
-        if i < n_right:
-            sr[i] = value.astype(BF)
-            send(sr.at[i], rr.at[i], kr + i, right)
-        else:
-            dkv[z] = value
-        if n_left and i < n_left:
-            value = dkv[zmod(z - n_left + i)]
-            if i:
-                recv(rl.at[i - 1], kl + i - 1)
-                value = value + rl[i - 1].astype(F32)
-            sl[i] = value.astype(BF)
-            send(sl.at[i], rl.at[i], kl + i, left)
-    if n_left:
-        recv(rl.at[n_left - 1], kl + n_left - 1)
-        dkv[z] += rl[n_left - 1].astype(F32)
+    kr, kl = alloc(2 * n_right), alloc(2 * max(n_left, 1))
     dx_s, dx_r = r["dx_s"], r["dx_r"]
     k_dx = alloc(1)
-    dx_s[...] = dkv[z, pl.ds(pl.multiple_of((1 - xl) * 128, 128), 128), :].astype(BF)
-    send(dx_s, dx_r, k_dx, cross)
+
+    def rows_of(xx):
+        return pl.ds(pl.multiple_of(xx * 128, 128), 128)
+
+    halves = ((0, 1 - xl), (1, xl))
+    for i in range(n_right + 1):
+        for half, xx in halves:
+            value = dkv[zmod(z + n_right - i), rows_of(xx), :]
+            if i:
+                recv(rr.at[half, i - 1], kr + 2 * (i - 1) + half)
+                value = value + rr[half, i - 1].astype(F32)
+            if i < n_right:
+                sr[half, i] = value.astype(BF)
+                send(sr.at[half, i], rr.at[half, i], kr + 2 * i + half, right)
+            elif half == 0:
+                if n_left:
+                    value = value + rl[half, n_left - 1].astype(F32)
+                dx_s[...] = value.astype(BF)
+                send(dx_s, dx_r, k_dx, cross)
+            else:
+                if n_left:
+                    value = value + rl[half, n_left - 1].astype(F32)
+                grad_kv = value
+        for half, xx in halves:
+            if n_left and i <= n_left:
+                if i:
+                    recv(rl.at[half, i - 1], kl + 2 * (i - 1) + half)
+                if i < n_left:
+                    value = dkv[zmod(z - n_left + i), rows_of(xx), :]
+                    if i:
+                        value = value + rl[half, i - 1].astype(F32)
+                    sl[half, i] = value.astype(BF)
+                    send(sl.at[half, i], rl.at[half, i], kl + 2 * i + half, left)
     recv(dx_r, k_dx)
-    grad_kv = dkv[z, pl.ds(pl.multiple_of(xl * 128, 128), 128), :] + dx_r[...].astype(F32)
+    grad_kv = grad_kv + dx_r[...].astype(F32)
 
     gg, inn, int_all = r["gg"], r["inn"], r["int_all"]
     pieces = [dq[h] for h in range(heads)]
     pieces += [(grad_kv[:, :128] * scale).astype(BF), grad_kv[:, 128:].astype(BF)]
     grads = jnp.concatenate(pieces, axis=1)
-    gg[s4] = grads
-    inn[s4] = row_tile(jnp.sum(grads.astype(F32) * cn[...], axis=1, keepdims=True))
-    k_gg, k_inn = alloc(4), alloc(4)
-    for k in range(1, 4):
-        to = dev(z, *near(k), t)
-        send(gg.at[s4], gg.at[s4], k_gg + k, to)
-        send(inn.at[s4], inn.at[s4], k_inn + k, to)
+    inn_tile = row_tile(jnp.sum(grads.astype(F32) * cn[...], axis=1, keepdims=True))
+    inn[s4] = inn_tile
+    marks = isel[...].astype(F32)
+    beside = (
+        jnp.sum(marks * inv[s4].T[:1], axis=1, keepdims=True),
+        jnp.sum(marks * inn_tile[:1], axis=1, keepdims=True),
+    )
+    lane = lax.broadcasted_iota(jnp.int32, (rows, 128), 1)
+    extra = jnp.zeros((rows, 128), F32)
+    for n, value in enumerate(beside):
+        for m in range(3):
+            part = value.astype(BF).astype(F32)
+            extra = jnp.where(lane == 3 * n + m, part, extra)
+            value = value - part
+    rall = r["rall"]
+    rall[z, xl, c] = jnp.concatenate([dot_nn(isel[...], grads).astype(BF), extra.astype(BF)], axis=1)
+    gather = Gather(lambda zz, xx, cc: rall.at[zz, xx, cc])
+
+    gg[s4] = dot_nn(tsel[s4], grads).astype(BF)
+    k_gg, k_inn = alloc(3), alloc(4)
+    send(gg.at[s4], gg.at[s4], k_gg, twin)
+    send(gg.at[s4], gg.at[s4], k_gg + 1, cross)
+    for k in range(1, 4):
+        send(inn.at[s4], inn.at[s4], k_inn + k, dev(z, *near(k), t))
+    gather.crossed()
+    across, corner = gg.at[(1 - xl) * 2 + c], gg.at[(1 - xl) * 2 + 1 - c]
+    recv(across, k_gg + 1)
+    send(across, across, k_gg + 2, twin)
     for k in range(1, 4):
         xx, cc = near(k)
-        recv(gg.at[xx * 2 + cc], k_gg + k)
         recv(inn.at[xx * 2 + cc], k_inn + k)
     int_all[t] = inn[...]
-    k_int, k_back = alloc(nt), alloc(nt)
+    k_int, k_back, k_int2, k_back2 = alloc(nt), alloc(nt), alloc(nt), alloc(nt)
     for d in range(1, nt):
         send(int_all.at[t], int_all.at[t], k_int + d, dev(z, xl, c, to_t(d)))
+    recv(gg.at[xl * 2 + 1 - c], k_gg)
+    recv(corner, k_gg + 2)
 
     bs, br, bo = r["bs"], r["br"], r["bo"]
+    depth_all = gg.shape[2]
 
     def back(d, carry):
         tt = to_t(d)
         block = dot_nt(
-            gg[...].reshape(plane, gg.shape[2]), wg[pl.ds(pl.multiple_of(tt * chunk, chunk), chunk), :]
+            gg[...].reshape(4 * texts, depth_all), wg[pl.ds(pl.multiple_of(tt * chunk, chunk), chunk), :]
         )
         bs[d] = block.astype(BF)
         rcopy(bs.at[d], br.at[d], k_back + d, dev(z, xl, c, tt)).start()
@@ -420,42 +528,80 @@
     lax.fori_loop(1, nt, back, 0)
     for d in range(1, nt):
         pending.append(rcopy(bs.at[d], br.at[d], k_back + d, dev(z, xl, c, to_t(d))))
-    bo[...] = dot_nt(gg[...].reshape(plane, gg.shape[2]), wg[pl.ds(pl.multiple_of(t * chunk, chunk), chunk), :])
+    for i in range(1, n_right + 1):
+        gather.step(i)
+        if i == 1:
+            bo[...] = dot_nt(
+                gg[...].reshape(4 * texts, depth_all), wg[pl.ds(pl.multiple_of(t * chunk, chunk), chunk), :]
+            )
+            own_x = dot_nn(h_own, r["outer_v"][t])
+            for d in range(1, nt):
+                recv(own_r.at[d], k_own + d)
+                own_x = own_x + own_r[d].astype(F32)
+            own_x = own_x.astype(BF).astype(F32)
+    gather.finish()
+
+    routed = dot_nn(wanted[...], rall[...].reshape(total, rall.shape[4]))
+    inv_row = routed[:, depth_all : depth_all + 1] + routed[:, depth_all + 1 : depth_all + 2]
+    inv_row = inv_row + routed[:, depth_all + 2 : depth_all + 3]
+    inn_row = routed[:, depth_all + 3 : depth_all + 4] + routed[:, depth_all + 4 : depth_all + 5]
+    inn_row = inn_row + routed[:, depth_all + 5 : depth_all + 6]
+    routed = routed[:, :depth_all].astype(BF)
+    int_own = r["int_own"]
+    int_own[t] = row_tile(inn_row)
+    bs2, br2 = r["bs2"], r["br2"]
+    for d in range(1, nt):
+        bs2[d] = dot_nt(routed, wg[pl.ds(pl.multiple_of(to_t(d) * chunk, chunk), chunk), :]).astype(BF)
+        send(bs2.at[d], br2.at[d], k_back2 + d, dev(z, xl, c, to_t(d)))
+        send(int_own.at[t], int_own.at[t], k_int2 + d, dev(z, xl, c, to_t(d)))
+    own_back = dot_nt(routed, wg[pl.ds(pl.multiple_of(t * chunk, chunk), chunk), :])
+
     for d in range(1, nt):
         recv(int_all.at[from_t(d)], k_int + d)
     for d in range(1, nt):
         recv(br.at[d], k_back + d)
         bo[...] += br[d].astype(F32)
-    gi, gt_s, gt_r = r["gi"], r["gt_s"], r["gt_r"]
+    gt_s, gt_r = r["gt_s"], r["gt_r"]
     for o in range(4):
         tile = int_all[0, o]
         for d in range(1, nt):
             tile = tile + int_all[d, o]
-        inv_o = inv[o][:, :1]
-        span = slice(o * 128, (o + 1) * 128)
-        x = xf[span, pl.ds(pl.multiple_of(t * chunk, chunk), chunk)].astype(F32)
-        grad = (inv_o * bo[span, :] - x * (inv_o * inv_o * column_of(tile)[:, :1] / width)).astype(BF)
-        gi[span, :] = grad
-        gt_s[o] = jnp.where(mask[span, :] > 0.5, jnp.zeros_like(grad), grad).reshape(2, 64, chunk)
-
-    k_gt = alloc(4)
+        marks = tsel[o].astype(F32)
+        inv_o = jnp.sum(marks * inv[o].T[:1], axis=1, keepdims=True)
+        inn_o = jnp.sum(marks * tile[:1], axis=1, keepdims=True)
+        x = dot_nn(tsel[o], xf[o * 128 : (o + 1) * 128, pl.ds(pl.multiple_of(t * chunk, chunk), chunk)])
+        grad = inv_o * bo[o * texts : (o + 1) * texts, :] - x * (inv_o * inv_o * inn_o / width)
+        gt_s[o] = dot_tn(tsel[o], grad.astype(BF)).astype(BF).reshape(2, 64, chunk)
+    k_gt, k_gr = alloc(4), alloc(4)
     for k in range(1, 4):
         xx, cc = near(k)
         send(gt_s.at[pl.ds(2 * xx, 2), cc], gt_r.at[s4], k_gt + k, dev(z, xx, cc, t))
-    rall = r["rall"]
-    gather_sec(rall, dot_tn(place[...], gi[...]).astype(BF), images)
-    wanted = jnp.where(r["gcol"][...] == lax.broadcasted_iota(jnp.int32, (rows, total), 1), 1.0, 0.0).astype(BF)
-    for xx in range(2):
-        for cc in range(2):
-            o = xx * 2 + cc
-            r["gimage"][:, o * chunk : (o + 1) * chunk] = dot_nn(wanted, rall[cc, xx]).astype(BF)
-
     gt_r[s4] = gt_s[pl.ds(2 * xl, 2), c]
+
+    for d in range(1, nt):
+        recv(int_own.at[from_t(d)], k_int2 + d)
+        recv(br2.at[d], k_back2 + d)
+        own_back = own_back + br2[d].astype(F32)
+    tile = int_own[0]
+    for d in range(1, nt):
+        tile = tile + int_own[d]
+    grad = inv_row * own_back - own_x * (inv_row * inv_row * column_of(tile)[:, :1] / width)
+    gr_s, gr_r = r["gr_s"], r["gr_r"]
+    gr_s[...] = grad.astype(BF).reshape(4, rows, chunk)
+    for k in range(1, 4):
+        xx, cc = near(k)
+        send(gr_s.at[xx * 2 + cc], gr_r.at[s4], k_gr + k, dev(z, xx, cc, t))
+    gr_r[s4] = gr_s[s4]
     for k in range(1, 4):
         xx, cc = near(k)
         recv(gt_r.at[xx * 2 + cc], k_gt + k)
     for o in range(4):
         r["gtext"][:, :, o * chunk : (o + 1) * chunk] = gt_r[o]
+    for k in range(1, 4):
+        xx, cc = near(k)
+        recv(gr_r.at[xx * 2 + cc], k_gr + k)
+    for o in range(4):
+        r["gimage"][:, o * chunk : (o + 1) * chunk] = gr_r[o]
     recv(att_r, k_att)
     r["attended"][c] = att_o[c]
     r["attended"][1 - c] = att_r[...]
@@ -479,7 +625,6 @@
 ):
     nsec, nt = lax.axis_size("sec"), lax.axis_size("tp")
     nz, ny = nsec // 4, max(nt // 2, 1)
-    sec = lax.axis_index("sec")
     rows, pw = patches.shape
     hid = merge_inner.shape[1]
     micro, tok, feat = text_embed.shape
@@ -492,22 +637,10 @@
     cols = (heads + 2) * HEAD_DIM
     plane = 512
 
-    batch, pos = slot_target // seq, slot_target % seq
-    key = (pos // 256) * plane + (pos // 128 % 2) * 256 + batch * 128 + pos % 128
-    rank = jnp.sum((key[None, :] < key[:, None]).astype(jnp.int32), axis=1)
-
-    def row_order(v):
-        return v.reshape(nz, 2, 2, rows).transpose(2, 1, 0, 3).reshape(1, total)
-
-    gcol = lax.dynamic_slice_in_dim(rank, sec * rows, rows).reshape(rows, 1)
-    my_gain = lax.dynamic_slice_in_dim(norm_gain, sec * depth, depth)[:, None]
-    weight = jnp.concatenate([query_weight, key_weight, value_weight], axis=1)
-    weight = (weight.astype(F32) * my_gain).astype(BF)
-
     vmem, anyspace = pl.BlockSpec(memory_space=pltpu.VMEM), pl.BlockSpec(memory_space=pl.ANY)
     n_right, n_left = nz // 2, max((nz - 1) // 2, 1)
-    n_sem = 192
-    ins = ["patches", "gain", "bias", "inner", "outer", "krow", "grow", "gcol", "text", "w", "cot"]
+    n_sem = 320
+    ins = ["patches", "gain", "bias", "inner", "outer", "slot", "ngain", "text", "wq", "wk", "wv", "cot"]
     outs = ["attended", "gtext", "gimage"]
     scratch = dict(
         pall=((nt, rows, pw), BF),
@@ -516,7 +649,20 @@
         a=((nt, 4, 2, tok, chunk), BF),
         wg=((nz * depth, cols), BF),
         d_out=((2, tok, heads * HEAD_DIM), BF),
-        hall=((2, 2, nz * rows, hid), BF),
+        w_v=((depth, cols), BF),
+        gain_v=((depth * nsec // 128, 128), F32),
+        kcol=((total, 128), F32),
+        wanted=((images, total), BF),
+        tsel=((4, 128 - rows, 128), BF),
+        isel=((rows, 128), BF),
+        own_s=((nt, images, chunk), BF),
+        own_r=((nt, images, chunk), BF),
+        int_own=((nt, 8, 128), F32),
+        bs2=((nt, images, chunk), BF),
+        br2=((nt, images, chunk), BF),
+        gr_s=((4, rows, chunk), BF),
+        gr_r=((4, rows, chunk), BF),
+        hall=((nz, 2, 2, rows, hid), BF),
         pick=((images, total), BF),
         place=((plane, images), BF),
         mask=((plane, chunk), F32),
@@ -527,8 +673,8 @@
         ss=((plane, 128), F32),
         ss_all=((4, 4, 8, 128), F32),
         inv=((4, 128, 128), F32),
-        c_s=((4, 128, cols), BF),
-        c_r=((4, 128, cols), BF),
+        c_s=((3, 128, cols), BF),
+        c_r=((3, 128, cols), BF),
         cn=((128, cols), F32),
         qs=((heads, 128, 128), BF),
         kv=((nz, 2, 128, 256), BF),
@@ -540,22 +686,21 @@
         att_o=((2, tok, heads * HEAD_DIM), BF),
         att_r=((tok, heads * HEAD_DIM), BF),
         dkv=((nz, 256, 256), F32),
-        sr=((n_right, 256, 256), BF),
-        rr=((n_right, 256, 256), BF),
-        sl=((n_left, 256, 256), BF),
-        rl=((n_left, 256, 256), BF),
+        sr=((2, n_right, 128, 256), BF),
+        rr=((2, n_right, 128, 256), BF),
+        sl=((2, n_left, 128, 256), BF),
+        rl=((2, n_left, 128, 256), BF),
         dx_s=((128, 256), BF),
         dx_r=((128, 256), BF),
-        gg=((4, 128, cols), BF),
+        gg=((4, 128 - rows, cols), BF),
         inn=((4, 8, 128), F32),
         int_all=((nt, 4, 8, 128), F32),
-        bs=((nt, plane, chunk), BF),
-        br=((nt, plane, chunk), BF),
-        bo=((plane, chunk), F32),
-        gi=((plane, chunk), BF),
+        bs=((nt, 4 * (128 - rows), chunk), BF),
+        br=((nt, 4 * (128 - rows), chunk), BF),
+        bo=((4 * (128 - rows), chunk), F32),
         gt_s=((4, 2, tok, chunk), BF),
         gt_r=((4, 2, tok, chunk), BF),
-        rall=((2, 2, nz * images, chunk), BF),
+        rall=((nz, 2, 2, rows, cols + 128), BF),
     )
     names = ins + outs + list(scratch) + ["ssem", "rsem", "lsem", "n_sem"]
     call = pl.pallas_call(
@@ -565,13 +710,13 @@
             jax.ShapeDtypeStruct((micro, tok, feat), BF),
             jax.ShapeDtypeStruct((rows, feat), BF),
         ),
-        in_specs=[anyspace if n in ("inner", "outer") else vmem for n in ins],
+        in_specs=[vmem if n in ("gain", "bias", "slot", "ngain") else anyspace for n in ins],
         out_specs=(vmem,) * 3,
         scratch_shapes=[pltpu.VMEM(shape, dtype) for shape, dtype in scratch.values()]
         + [
             pltpu.SemaphoreType.DMA((n_sem,)),
             pltpu.SemaphoreType.DMA((n_sem,)),
-            pltpu.SemaphoreType.DMA((16,)),
+            pltpu.SemaphoreType.DMA((24,)),
         ],
         compiler_params=pltpu.CompilerParams(
             collective_id=0, has_side_effects=True, vmem_limit_bytes=56 * 1024 * 1024
@@ -580,15 +725,16 @@
     )
     return call(
         patches,
-        merge_gain.reshape(1, -1),
-        merge_bias.reshape(1, -1),
+        merge_gain,
+        merge_bias,
         merge_inner,
         merge_outer,
-        row_order(key),
-        row_order(rank),
-        gcol,
+        slot_target,
+        norm_gain,
         text_embed,
-        weight,
+        query_weight,
+        key_weight,
+        value_weight,
         attn_cotangent,
     )
 

time: 224 us -> 167 us (0.75)
  Pallas kernels: 207 us -> 161 us
  local copies, waits for them, and re-layouts: 10.3 us -> 4.71 us
  other arithmetic: 3.17 us -> 0 us
    pallas_call x1, Pallas kernels: 207 us -> 161 us  [per_device(): call(patches, merge_gain, merge_bias, merge_inner, merge_outer, slot_targ...]
    reshape x8 -> x0, local copies, waits for them, and re-layouts: 4.85 us -> none  [the longest x4 1.5 us: row_order(): return v.reshape(nz, 2, 2, rows).transpose(2, 1, 0, 3).reshape(1, total)]
where the time goes in v2:
time: 167 us
  Pallas kernels  161 us (96%)
  local copies, waits for them, and re-layouts  4.71 us (3%)
    pallas_call x1, Pallas kernels, per_device(): call(patches, merge_gain, merge_bias, merge_inner, merge_outer, slot_targ...  161 us
    unnamed x3, local copies, waits for them, and re-layouts  4.71 us

profile of v2, /device:TPU:1, one launch (start us, length us, event | category | flops | bytes accessed | tf_op | source)
XLA Modules:
  0.0 166.6 jit_solution(1613653424419771369)
XLA Ops:
  0.6 161.2 %merged_step.1 = (bf16[2,64,512]{2,1,0:T(8,128)(2,1)}, bf16[2,64,1024]{2,1,0:T(8,128)(2,1)}, bf16[32,1024]{1,0:T(8,128)(2,1)}) custom-call(bf16[32,640]{1,0:T(8,128)(2,1)} %refs_0_.1, f32[1280]{0:T(1024)} %refs_1_.1, f32[1280]{0:T(1024)} %refs_2_.1, bf16[5120,384]{1,0:T(8,128)(2,1)} %refs_3_.1, bf16[384,8192]{1,0:T(8,128)(2,1)} %refs_4_.1, s32[1024]{0:T(1024)} %refs_5_.1, ...), custom_call_target="tpu_custom_call" | custom-call | tf_op jit(solution)/shard_map/merged_step/pallas_call | solution.py:726
  161.9 1.6 copy.18
  163.4 1.7 %copy.19 = bf16[2,64,1024]{2,1,0:T(8,128)(2,1)} copy(bf16[2,64,1024]{2,1,0:T(8,128)(2,1)} %get-tuple-element.7) | data formatting | bytes 524288
  165.1 1.5 copy.20

commit v3 on v2

--- a/solution.py
+++ b/solution.py
@@ -12,8 +12,6 @@
 BF = jnp.bfloat16
 F32 = jnp.float32
 MESH = pl.DeviceIdType.MESH
-TEXT_AT = 2
-W_AT = 2
 
 
 def dot_nn(a, b):
@@ -227,18 +225,19 @@
         recv(a_ref.at[t, pl.ds(2 * xx, 2), cc], k_text + k)
     k_a = alloc(nt)
 
-    def text_out():
-        for d in range(1, nt):
-            send(a_ref.at[t], a_ref.at[t], k_a + d, dev(z, xl, c, to_t(d)))
-
-    if TEXT_AT == 0:
-        text_out()
+    across_x = range(ny, nt, ny)
+    for d in [*range(1, ny), *across_x]:
+        send(a_ref.at[t], a_ref.at[t], k_a + d, dev(z, xl, c, to_t(d)))
+
+    def text_on():
+        for first in across_x:
+            ref = a_ref.at[from_t(first)]
+            recv(ref, k_a + first)
+            for d in range(1, ny):
+                send(ref, ref, k_a + first + d, dev(z, xl, c, to_t(d)))
+
     for d in range(1, nt):
         recv(pall.at[from_t(d)], k_patch + d)
-    if TEXT_AT == 1:
-        text_out()
-    if W_AT == 1:
-        ring_w.step(1)
     inner_copy.wait()
     vit = gain.shape[0]
     per = vit // pw
@@ -285,19 +284,15 @@
 
     hall = r["hall"]
     hall[z, xl, c] = hidden
-    if W_AT == 2:
-        ring_w.step(1)
+    ring_w.step(1)
     gather = Gather(lambda zz, xx, cc: hall.at[zz, xx, cc])
     gather.crossed()
-    if TEXT_AT == 2:
-        text_out()
+    text_on()
     for i in range(1, n_right + 1):
         gather.step(i)
     gather.finish()
     if n_right > 2:
         ring_w.step(2)
-    if TEXT_AT == 3:
-        text_out()
 
     hp = dot_nn(pick[...], hall[...].reshape(total, hall.shape[4])).astype(BF)
     for copy in outer_copies:
@@ -329,7 +324,10 @@
     ss[...] = take(t)
 
     def take_next(d, carry):
-        recv(a_ref.at[from_t(d)], k_a + d)
+        @pl.when(lax.rem(d, ny) != 0)
+        def _():
+            recv(a_ref.at[from_t(d)], k_a + d)
+
         recv(img.at[from_t(d)], k_img + d)
         ss[...] += take(from_t(d))
         return carry
@@ -421,28 +419,28 @@
     k_att = alloc(1)
     send(att_o.at[1 - c], att_r, k_att, twin)
 
-    dkv = r["dkv"]
-
-    def key_block(zz, carry):
-        lanes = pl.ds(pl.multiple_of(zz * 256, 256), 256)
-        dkv[zz, :, :128] = dot_tn(ds[:, :, lanes].reshape(heads * 128, 256), qs[...].reshape(heads * 128, 128))
-        dkv[zz, :, 128:] = dot_tn(ph[:, :, lanes].reshape(heads * 128, 256), dos[...].reshape(heads * 128, 128))
-        return carry
-
-    lax.fori_loop(0, nz, key_block, 0)
-
     sr, rr, sl, rl = r["sr"], r["rr"], r["sl"], r["rl"]
     kr, kl = alloc(2 * n_right), alloc(2 * max(n_left, 1))
     dx_s, dx_r = r["dx_s"], r["dx_r"]
     k_dx = alloc(1)
 
-    def rows_of(xx):
-        return pl.ds(pl.multiple_of(xx * 128, 128), 128)
-
+    def make(n, carry):
+        zz, xx = lax.rem(z + n_right + lax.div(n, 2), nz), lax.rem(n, 2)
+        lanes = pl.ds(pl.multiple_of((zz * 2 + xx) * 128, 128), 128)
+        grad_keys = dot_tn(ds[:, :, lanes].reshape(heads * 128, 128), qs[...].reshape(heads * 128, 128))
+        grad_values = dot_tn(ph[:, :, lanes].reshape(heads * 128, 128), dos[...].reshape(heads * 128, 128))
+        dkv[zz, xx, :, :128] = grad_keys
+        dkv[zz, xx, :, 128:] = grad_values
+        return carry
+
+    dkv = r["dkv"]
+    lax.fori_loop(0, 4, make, 0)
     halves = ((0, 1 - xl), (1, xl))
     for i in range(n_right + 1):
+        if i == 1:
+            lax.fori_loop(4, 2 * nz, make, 0)
         for half, xx in halves:
-            value = dkv[zmod(z + n_right - i), rows_of(xx), :]
+            value = dkv[zmod(z + n_right - i), xx]
             if i:
                 recv(rr.at[half, i - 1], kr + 2 * (i - 1) + half)
                 value = value + rr[half, i - 1].astype(F32)
@@ -463,7 +461,7 @@
                 if i:
                     recv(rl.at[half, i - 1], kl + 2 * (i - 1) + half)
                 if i < n_left:
-                    value = dkv[zmod(z - n_left + i), rows_of(xx), :]
+                    value = dkv[zmod(z - n_left + i), xx]
                     if i:
                         value = value + rl[half, i - 1].astype(F32)
                     sl[half, i] = value.astype(BF)
@@ -499,6 +497,29 @@
     send(gg.at[s4], gg.at[s4], k_gg + 1, cross)
     for k in range(1, 4):
         send(inn.at[s4], inn.at[s4], k_inn + k, dev(z, *near(k), t))
+    k_int, k_back, k_int2, k_back2 = alloc(nt), alloc(2 * nt), alloc(nt), alloc(nt)
+
+    bs, br, bo = r["bs"], r["br"], r["bo"]
+    depth_all = gg.shape[2]
+
+    def back(half, xx):
+        def one(tt):
+            lines = gg[pl.ds(2 * xx, 2)].reshape(2 * texts, depth_all)
+            return dot_nt(lines, wg[pl.ds(pl.multiple_of(tt * chunk, chunk), chunk), :])
+
+        def step(d, carry):
+            tt = to_t(d)
+            bs[d, xx] = one(tt).astype(BF)
+            rcopy(bs.at[d, xx], br.at[d, xx], k_back + 2 * d + half, dev(z, xl, c, tt)).start()
+            return carry
+
+        lax.fori_loop(1, nt, step, 0)
+        for d in range(1, nt):
+            pending.append(rcopy(bs.at[d, xx], br.at[d, xx], k_back + 2 * d + half, dev(z, xl, c, to_t(d))))
+        return one
+
+    recv(gg.at[xl * 2 + 1 - c], k_gg)
+    near_half = back(0, xl)
     gather.crossed()
     across, corner = gg.at[(1 - xl) * 2 + c], gg.at[(1 - xl) * 2 + 1 - c]
     recv(across, k_gg + 1)
@@ -507,33 +528,15 @@
         xx, cc = near(k)
         recv(inn.at[xx * 2 + cc], k_inn + k)
     int_all[t] = inn[...]
-    k_int, k_back, k_int2, k_back2 = alloc(nt), alloc(nt), alloc(nt), alloc(nt)
     for d in range(1, nt):
         send(int_all.at[t], int_all.at[t], k_int + d, dev(z, xl, c, to_t(d)))
-    recv(gg.at[xl * 2 + 1 - c], k_gg)
     recv(corner, k_gg + 2)
-
-    bs, br, bo = r["bs"], r["br"], r["bo"]
-    depth_all = gg.shape[2]
-
-    def back(d, carry):
-        tt = to_t(d)
-        block = dot_nt(
-            gg[...].reshape(4 * texts, depth_all), wg[pl.ds(pl.multiple_of(tt * chunk, chunk), chunk), :]
-        )
-        bs[d] = block.astype(BF)
-        rcopy(bs.at[d], br.at[d], k_back + d, dev(z, xl, c, tt)).start()
-        return carry
-
-    lax.fori_loop(1, nt, back, 0)
-    for d in range(1, nt):
-        pending.append(rcopy(bs.at[d], br.at[d], k_back + d, dev(z, xl, c, to_t(d))))
+    far_half = back(1, 1 - xl)
     for i in range(1, n_right + 1):
         gather.step(i)
         if i == 1:
-            bo[...] = dot_nt(
-                gg[...].reshape(4 * texts, depth_all), wg[pl.ds(pl.multiple_of(t * chunk, chunk), chunk), :]
-            )
+            bo[xl] = near_half(t)
+            bo[1 - xl] = far_half(t)
             own_x = dot_nn(h_own, r["outer_v"][t])
             for d in range(1, nt):
                 recv(own_r.at[d], k_own + d)
@@ -559,7 +562,8 @@
     for d in range(1, nt):
         recv(int_all.at[from_t(d)], k_int + d)
     for d in range(1, nt):
-        recv(br.at[d], k_back + d)
+        for half, xx in ((0, xl), (1, 1 - xl)):
+            recv(br.at[d, xx], k_back + 2 * d + half)
         bo[...] += br[d].astype(F32)
     gt_s, gt_r = r["gt_s"], r["gt_r"]
     for o in range(4):
@@ -570,7 +574,7 @@
         inv_o = jnp.sum(marks * inv[o].T[:1], axis=1, keepdims=True)
         inn_o = jnp.sum(marks * tile[:1], axis=1, keepdims=True)
         x = dot_nn(tsel[o], xf[o * 128 : (o + 1) * 128, pl.ds(pl.multiple_of(t * chunk, chunk), chunk)])
-        grad = inv_o * bo[o * texts : (o + 1) * texts, :] - x * (inv_o * inv_o * inn_o / width)
+        grad = inv_o * bo[o // 2, o % 2 * texts : (o % 2 + 1) * texts, :] - x * (inv_o * inv_o * inn_o / width)
         gt_s[o] = dot_tn(tsel[o], grad.astype(BF)).astype(BF).reshape(2, 64, chunk)
     k_gt, k_gr = alloc(4), alloc(4)
     for k in range(1, 4):
@@ -685,19 +689,19 @@
         dq=((heads, 128, 128), BF),
         att_o=((2, tok, heads * HEAD_DIM), BF),
         att_r=((tok, heads * HEAD_DIM), BF),
-        dkv=((nz, 256, 256), F32),
         sr=((2, n_right, 128, 256), BF),
         rr=((2, n_right, 128, 256), BF),
         sl=((2, n_left, 128, 256), BF),
         rl=((2, n_left, 128, 256), BF),
+        dkv=((nz, 2, 128, 256), F32),
         dx_s=((128, 256), BF),
         dx_r=((128, 256), BF),
         gg=((4, 128 - rows, cols), BF),
         inn=((4, 8, 128), F32),
         int_all=((nt, 4, 8, 128), F32),
-        bs=((nt, 4 * (128 - rows), chunk), BF),
-        br=((nt, 4 * (128 - rows), chunk), BF),
-        bo=((4 * (128 - rows), chunk), F32),
+        bs=((nt, 2, 2 * (128 - rows), chunk), BF),
+        br=((nt, 2, 2 * (128 - rows), chunk), BF),
+        bo=((2, 2 * (128 - rows), chunk), F32),
         gt_s=((4, 2, tok, chunk), BF),
         gt_r=((4, 2, tok, chunk), BF),
         rall=((nz, 2, 2, rows, cols + 128), BF),

time: 167 us -> 164 us (0.982)
  Pallas kernels: 161 us -> 158 us
    pallas_call x1, Pallas kernels: 161 us -> 158 us  [per_device(): call(patches, merge_gain, merge_bias, merge_inner, merge_outer, slot_targ...]
where the time goes in v3:
time: 164 us; the launch traced here: 163 us
  Pallas kernels  158 us (96%)
  local copies, waits for them, and re-layouts  4.71 us (3%)
    pallas_call x1, Pallas kernels, per_device(): call(patches, merge_gain, merge_bias, merge_inner, merge_outer, slot_targ...  158 us
    unnamed x3, local copies, waits for them, and re-layouts  4.71 us

profile of v3, /device:TPU:1, one launch (start us, length us, event | category | flops | bytes accessed | tf_op | source)
XLA Modules:
  0.0 162.9 jit_solution(1057252350749702008)
XLA Ops:
  0.6 157.5 %merged_step.1 = (bf16[2,64,512]{2,1,0:T(8,128)(2,1)}, bf16[2,64,1024]{2,1,0:T(8,128)(2,1)}, bf16[32,1024]{1,0:T(8,128)(2,1)}) custom-call(bf16[32,640]{1,0:T(8,128)(2,1)} %refs_0_.1, f32[1280]{0:T(1024)} %refs_1_.1, f32[1280]{0:T(1024)} %refs_2_.1, bf16[5120,384]{1,0:T(8,128)(2,1)} %refs_3_.1, bf16[384,8192]{1,0:T(8,128)(2,1)} %refs_4_.1, s32[1024]{0:T(1024)} %refs_5_.1, ...), custom_call_target="tpu_custom_call" | custom-call | tf_op jit(solution)/shard_map/merged_step/pallas_call | solution.py:730
  158.2 1.6 copy.18
  159.8 1.7 %copy.19 = bf16[2,64,1024]{2,1,0:T(8,128)(2,1)} copy(bf16[2,64,1024]{2,1,0:T(8,128)(2,1)} %get-tuple-element.7) | data formatting | bytes 524288
  161.4 1.5 copy.20

commit v4 on v3

--- a/solution.py
+++ b/solution.py
@@ -62,6 +62,8 @@
     def from_t(d):
         dx, dy = d // ny, d % ny
         return lax.rem(xh + nxh - dx, nxh) * ny + lax.rem(y + ny - dy, ny)
+
+    around = [ny * (1 - n % 2) + (n + 1) // 2 for n in range(nt - 1)]
 
     def near(k):
         a = 1 - xl if k // 2 else xl
@@ -299,7 +301,7 @@
         copy.wait()
     part_s, part_r, img = r["part_s"], r["part_r"], r["img"]
     k_part, k_img = alloc(nt), alloc(nt)
-    for d in range(1, nt):
+    for d in around:
         part_s[d] = dot_nn(hp, r["outer_v"][to_t(d)]).astype(BF)
         send(part_s.at[d], part_r.at[d], k_part + d, dev(z, xl, c, to_t(d)))
     mine = dot_nn(hp, r["outer_v"][t])
@@ -307,7 +309,7 @@
         recv(part_r.at[d], k_part + d)
         mine = mine + part_r[d].astype(F32)
     img[t] = mine.astype(BF)
-    for d in range(1, nt):
+    for d in around:
         send(img.at[t], img.at[t], k_img + d, dev(z, xl, c, to_t(d)))
     if n_right > 3:
         ring_w.step(3)
@@ -382,7 +384,7 @@
     own_s, own_r = r["own_s"], r["own_r"]
     k_own = alloc(nt)
     h_own = hall[z].reshape(images, hall.shape[4])
-    for d in range(1, nt):
+    for d in around:
         own_s[d] = dot_nn(h_own, r["outer_v"][to_t(d)]).astype(BF)
         send(own_s.at[d], own_r.at[d], k_own + d, dev(z, xl, c, to_t(d)))
     recv(d_out.at[1 - c], k_cot)
@@ -401,7 +403,7 @@
         query_pos = z * 256 + xl * 128 + lax.broadcasted_iota(jnp.int32, (128, seq), 0)
         scores = jnp.where(lax.broadcasted_iota(jnp.int32, (128, seq), 1) <= query_pos, scores, -1e30)
         raw = jnp.exp(scores - jnp.max(scores, axis=1, keepdims=True))
-        probs = raw / jnp.sum(raw, axis=1, keepdims=True)
+        probs = raw * (1.0 / jnp.sum(raw, axis=1, keepdims=True))
         half = probs.astype(BF)
         ph[h] = half
         att[h] = dot_nn(half, values).astype(BF)
@@ -412,7 +414,7 @@
         dq[h] = (dot_nn(grad, keys) * scale).astype(BF)
         return carry
 
-    lax.fori_loop(0, heads, head, 0)
+    lax.fori_loop(0, heads, head, 0, unroll=2)
     att_o, att_r = r["att_o"], r["att_r"]
     for h in range(heads):
         att_o[:, :, h * 128 : (h + 1) * 128] = att[h].reshape(2, 64, 128)
@@ -507,13 +509,14 @@
             lines = gg[pl.ds(2 * xx, 2)].reshape(2 * texts, depth_all)
             return dot_nt(lines, wg[pl.ds(pl.multiple_of(tt * chunk, chunk), chunk), :])
 
-        def step(d, carry):
+        def step(n, carry):
+            d = ny * (1 - n % 2) + (n + 1) // 2
             tt = to_t(d)
             bs[d, xx] = one(tt).astype(BF)
             rcopy(bs.at[d, xx], br.at[d, xx], k_back + 2 * d + half, dev(z, xl, c, tt)).start()
             return carry
 
-        lax.fori_loop(1, nt, step, 0)
+        lax.fori_loop(0, nt - 1, step, 0)
         for d in range(1, nt):
             pending.append(rcopy(bs.at[d, xx], br.at[d, xx], k_back + 2 * d + half, dev(z, xl, c, to_t(d))))
         return one
@@ -553,7 +556,7 @@
     int_own = r["int_own"]
     int_own[t] = row_tile(inn_row)
     bs2, br2 = r["bs2"], r["br2"]
-    for d in range(1, nt):
+    for d in around:
         bs2[d] = dot_nt(routed, wg[pl.ds(pl.multiple_of(to_t(d) * chunk, chunk), chunk), :]).astype(BF)
         send(bs2.at[d], br2.at[d], k_back2 + d, dev(z, xl, c, to_t(d)))
         send(int_own.at[t], int_own.at[t], k_int2 + d, dev(z, xl, c, to_t(d)))

time: 164 us -> 163 us (level)
  no operation moved by 1% of the time
where the time goes in v4:
time: 163 us
  Pallas kernels  158 us (97%)
  local copies, waits for them, and re-layouts  4.71 us (3%)
    pallas_call x1, Pallas kernels, per_device(): call(patches, merge_gain, merge_bias, merge_inner, merge_outer, slot_targ...  158 us
    unnamed x3, local copies, waits for them, and re-layouts  4.71 us

profile of v4, /device:TPU:1, one launch (start us, length us, event | category | flops | bytes accessed | tf_op | source)
XLA Modules:
  0.0 163.2 jit_solution(10636412139861654322)
XLA Ops:
  0.6 157.9 %merged_step.1 = (bf16[2,64,512]{2,1,0:T(8,128)(2,1)}, bf16[2,64,1024]{2,1,0:T(8,128)(2,1)}, bf16[32,1024]{1,0:T(8,128)(2,1)}) custom-call(bf16[32,640]{1,0:T(8,128)(2,1)} %refs_0_.1, f32[1280]{0:T(1024)} %refs_1_.1, f32[1280]{0:T(1024)} %refs_2_.1, bf16[5120,384]{1,0:T(8,128)(2,1)} %refs_3_.1, bf16[384,8192]{1,0:T(8,128)(2,1)} %refs_4_.1, s32[1024]{0:T(1024)} %refs_5_.1, ...), custom_call_target="tpu_custom_call" | custom-call | tf_op jit(solution)/shard_map/merged_step/pallas_call | solution.py:733
  158.5 1.6 copy.18
  160.1 1.7 %copy.19 = bf16[2,64,1024]{2,1,0:T(8,128)(2,1)} copy(bf16[2,64,1024]{2,1,0:T(8,128)(2,1)} %get-tuple-element.7) | data formatting | bytes 524288
  161.8 1.5 copy.20

commit v5 on v4

--- a/solution.py
+++ b/solution.py
@@ -414,7 +414,7 @@
         dq[h] = (dot_nn(grad, keys) * scale).astype(BF)
         return carry
 
-    lax.fori_loop(0, heads, head, 0, unroll=2)
+    lax.fori_loop(0, heads, head, 0, unroll=4)
     att_o, att_r = r["att_o"], r["att_r"]
     for h in range(heads):
         att_o[:, :, h * 128 : (h + 1) * 128] = att[h].reshape(2, 64, 128)

time: 163 us -> 164 us (level)
  no operation moved by 1% of the time
where the time goes in v5:
time: 164 us; the launch traced here: 163 us
  Pallas kernels  158 us (96%)
  local copies, waits for them, and re-layouts  4.71 us (3%)
    pallas_call x1, Pallas kernels, per_device(): call(patches, merge_gain, merge_bias, merge_inner, merge_outer, slot_targ...  158 us
    unnamed x3, local copies, waits for them, and re-layouts  4.71 us

profile of v5, /device:TPU:1, one launch (start us, length us, event | category | flops | bytes accessed | tf_op | source)
XLA Modules:
  0.0 163.3 jit_solution(9603661793458571353)
XLA Ops:
  0.6 157.9 %merged_step.1 = (bf16[2,64,512]{2,1,0:T(8,128)(2,1)}, bf16[2,64,1024]{2,1,0:T(8,128)(2,1)}, bf16[32,1024]{1,0:T(8,128)(2,1)}) custom-call(bf16[32,640]{1,0:T(8,128)(2,1)} %refs_0_.1, f32[1280]{0:T(1024)} %refs_1_.1, f32[1280]{0:T(1024)} %refs_2_.1, bf16[5120,384]{1,0:T(8,128)(2,1)} %refs_3_.1, bf16[384,8192]{1,0:T(8,128)(2,1)} %refs_4_.1, s32[1024]{0:T(1024)} %refs_5_.1, ...), custom_call_target="tpu_custom_call" | custom-call | tf_op jit(solution)/shard_map/merged_step/pallas_call | solution.py:733
  158.5 1.6 copy.18
  160.1 1.7 %copy.19 = bf16[2,64,1024]{2,1,0:T(8,128)(2,1)} copy(bf16[2,64,1024]{2,1,0:T(8,128)(2,1)} %get-tuple-element.7) | data formatting | bytes 524288
  161.8 1.5 copy.20
